TPU v7x, 256 devices: a whole 4x4x8 slice. The times are simulated.
256 devices in a mesh: dp: 8 (over x, core), expert: 32 (over z, y).
Axes of the slice: x: 4, y: 4, z: 8, core: 2. Of those that a mesh axis runs over, the one named last changes fastest.
Arguments:
- grad_out: bfloat16 [32768, 3584], P(('dp', 'expert')), may hold values from -1.5 to 1.5
- gate_probs: float32 [32768, 4], P(('dp', 'expert')), may hold values from 0.05 to 0.3
- expert_route: int32 [32768, 4], P(('dp', 'expert')), may hold values from 0 to 23, all different within a row; in each aligned block of 128 rows (0 to 127, 128 to 255, ...) at most 24 rows name the same one
- replica_pick: int32 [32768, 4], P(('dp', 'expert')), may hold values from 0 to 59
- slot_expert: int32 [32], replicated, may hold values from 0 to 23, as said below
- saved_hidden: bfloat16 [8, 32, 32, 1, 24, 1024], P('dp', 'expert'), may hold values from -6 to 6
- master: float32 [32, 1024, 3584], P('expert', 'dp'), as said below
- first_moment: bfloat16 [32, 1024, 3584], P('expert', 'dp'), as said below
- second_moment: bfloat16 [32, 1024, 3584], P('expert', 'dp'), as said below
Outputs:
- hidden_grad: bfloat16 [8, 32, 32, 1, 24, 1024], P('dp', 'expert')
- gate_grad: float32 [32768, 4], P(('dp', 'expert'))
- new_master: float32 [32, 1024, 3584], P('expert', 'dp')
- new_first: bfloat16 [32, 1024, 3584], P('expert', 'dp')
- new_second: bfloat16 [32, 1024, 3584], P('expert', 'dp')
Inputs may be any that keep to these rules, and one draw needn't show every extreme that they name: `expert_route`: each row names 4 different experts; in the rows of one device no expert is named more than 24 times, a bound that some block reaches. `slot_expert`: every expert has at least one slot; experts 0 to 2 have two or more slots each, every other expert exactly one. `master`: slots holding the same expert hold equal values. `first_moment`: slots holding the same expert hold equal values. `second_moment`: slots holding the same expert hold equal values; all entries are positive.
All inputs are finite; a program needn't handle non-finite values.
Results may differ from a plain program's by a relative error of at most 0.017.
Values may be sent and summed in bfloat16 or wider, within the bound.
A program may use at most 128 MiB of HBM per device.

v0:
```python
import jax
import jax.numpy as jnp
from jax import lax
from jax.sharding import PartitionSpec as P

HOT = 3


beta_one = 0.9
beta_two = 0.95
learn_rate = 0.00022
decay_rate = 0.1
epsilon = 1e-08
correct_one = 0.6513215599
correct_two = 0.4012630607


def on_device(
    grad_out,
    gate_probs,
    expert_route,
    replica_pick,
    slot_expert,
    saved_hidden,
    master,
    first_moment,
    second_moment,
):
    dev_count = lax.axis_size("expert")
    slot_count = slot_expert.shape[0]
    slot_dev = slot_count // dev_count
    capacity = saved_hidden.shape[4]
    feature_count = grad_out.shape[1]
    tok_rows, top_count = gate_probs.shape
    assigned = tok_rows * top_count
    shard_rows = master.shape[1]
    slot_ids = jnp.arange(slot_count, dtype=jnp.int32)
    same_expert = slot_expert[:, None] == slot_expert[None, :]
    slot_rank = jnp.sum(same_expert & (slot_ids[None, :] < slot_ids[:, None]), axis=1)
    experts_flat = expert_route.reshape(assigned)
    replica_picks = replica_pick.reshape(assigned)
    host_mask = slot_expert[None, :] == experts_flat[:, None]
    copy_count = jnp.sum(host_mask.astype(jnp.int32), axis=1)
    chosen = host_mask & (slot_rank[None, :] == (replica_picks % copy_count)[:, None])
    target = jnp.sum(jnp.where(chosen, slot_ids[None, :], 0), axis=1)
    onehot = (target[:, None] == slot_ids[None, :]).astype(jnp.int32)
    position = jnp.sum(onehot * (jnp.cumsum(onehot, axis=0) - onehot), axis=1)
    dest_index = target * capacity + position
    repeated = jnp.repeat(grad_out, top_count, axis=0)
    send_rows = (
        jnp.zeros((slot_count * capacity, feature_count), jnp.bfloat16).at[dest_index].set(repeated)
    )
    send_gates = (
        jnp.zeros((slot_count * capacity,), jnp.bfloat16)
        .at[dest_index]
        .set(gate_probs.reshape(assigned).astype(jnp.bfloat16))
    )
    recv_rows, recv_gates = (
        lax.all_to_all(
            send_rows.reshape(dev_count, slot_dev, capacity, feature_count),
            "expert",
            split_axis=0,
            concat_axis=0,
            tiled=True,
        ),
        lax.all_to_all(
            send_gates.reshape(dev_count, slot_dev, capacity),
            "expert",
            split_axis=0,
            concat_axis=0,
            tiled=True,
        ),
    )
    hidden = saved_hidden[0, 0]
    weights = master.astype(jnp.bfloat16)
    projected = jnp.einsum(
        "qlcd,lhd->qlch",
        recv_rows,
        lax.all_gather(weights, "dp", axis=1, tiled=True),
        preferred_element_type=jnp.float32,
    )
    gate_scale = recv_gates.astype(jnp.float32)[..., None]
    hidden_grad = (gate_scale * projected).astype(jnp.bfloat16)
    gate_terms = jnp.sum(hidden.astype(jnp.float32) * projected, axis=-1)
    returned = lax.all_to_all(gate_terms, "expert", split_axis=0, concat_axis=0, tiled=True)
    gate_grad = returned.reshape(slot_count * capacity)[dest_index].reshape(tok_rows, top_count)
    scaled = (gate_scale * recv_rows.astype(jnp.float32)).astype(jnp.bfloat16)
    reduced = lax.psum_scatter(
        jnp.einsum("qlch,qlcd->hld", hidden, scaled, preferred_element_type=jnp.float32).astype(
            jnp.bfloat16
        ),
        "dp",
        scatter_dimension=0,
        tiled=True,
    ).astype(jnp.float32)
    local_grad = jnp.transpose(reduced, (1, 0, 2))
    flat_grad = local_grad.reshape(slot_dev, shard_rows * feature_count)
    own_slots = lax.dynamic_slice_in_dim(slot_expert, lax.axis_index("expert") * slot_dev, slot_dev)
    hot_ids = jnp.arange(HOT, dtype=jnp.int32)
    hot_hit = (own_slots[:, None] == hot_ids[None, :]).astype(jnp.float32)
    grad_table = jnp.dot(hot_hit.T, flat_grad, precision=lax.Precision.HIGHEST)
    grad_table = lax.psum(grad_table.astype(jnp.bfloat16), "expert").astype(jnp.float32)
    hot_flag = jnp.sum(hot_hit, axis=1, keepdims=True)
    grad_flat = (
        jnp.dot(hot_hit, grad_table, precision=lax.Precision.HIGHEST) + (1.0 - hot_flag) * flat_grad
    )
    grad_total = grad_flat.reshape(local_grad.shape)
    new_first = beta_one * first_moment.astype(jnp.float32) + (1.0 - beta_one) * grad_total
    new_second = (
        beta_two * second_moment.astype(jnp.float32) + (1.0 - beta_two) * grad_total * grad_total
    )
    update = (
        new_first / correct_one / (jnp.sqrt(new_second / correct_two) + epsilon)
        + decay_rate * master
    )
    new_master = master - learn_rate * update
    return (
        hidden_grad[None, None],
        gate_grad,
        new_master,
        new_first.astype(jnp.bfloat16),
        new_second.astype(jnp.bfloat16),
    )


def solution(mesh):
    placed = (
        P(("dp", "expert"), None),
        P(("dp", "expert"), None),
        P(("dp", "expert"), None),
        P(("dp", "expert"), None),
        P(),
        P("dp", "expert", None, None, None, None),
        P("expert", "dp", None),
        P("expert", "dp", None),
        P("expert", "dp", None),
    )
    return jax.shard_map(
        on_device,
        mesh=mesh,
        in_specs=placed,
        out_specs=(
            P("dp", "expert", None, None, None, None),
            P(("dp", "expert"), None),
            P("expert", "dp", None),
            P("expert", "dp", None),
            P("expert", "dp", None),
        ),
        check_vma=False,
    )
```

profile of v0, /device:TPU:2, one launch (start us, length us, event | category | flops | bytes accessed | tf_op | source)
XLA Modules:
  0.0 527.3 jit_solution(3965733811564665236)
XLA Ops:
  7.2 0.8 copy.39
  8.0 0.1 eq.105
  8.1 0.9 convert_reduce_fusion
  9.0 0.8 fusion.16
  9.7 0.8 copy.40
  10.5 0.1 reshape.220
  10.6 0.1 add_select_fusion
  10.8 0.7 select_reduce_fusion
  11.5 1.2 reduce-window.6
  12.7 0.2 slice_reduce_fusion
  12.9 0.1 fusion.19
  13.1 0.7 convert_element_type.89
  13.8 0.1 copy.42
  13.9 0.1 reshape.250
  14.0 3.8 scatter_custom_fusion
  17.8 0.7 reshape.266
  18.5 11.7 %all-to-all-start = ((bf16[32,1,24]{2,1,0:T(2,128)(2,1)}), bf16[32,1,24]{2,1,0:T(2,128)(2,1)S(1)}, u32[]{:S(2)}, u32[]{:S(2)}) async-start(bf16[32,1,24]{2,1,0:T(2,128)(2,1)} %reshape.266), calls=%async_computation | async-start | bytes 32768 | tf_op jit(solution)/shard_map/all_to_all | solution.py:66
  30.2 3.9 broadcast_in_dim.56
  34.1 6.7 %reshape.258 = bf16[512,3584]{1,0:T(8,128)(2,1)} reshape(bf16[128,4,3584]{2,1,0:T(4,128)(2,1)} %broadcast_in_dim.56) | data formatting | bytes 7340032 | tf_op jit(solution)/shard_map/reshape | solution.py:49
  40.8 10.2 %scatter_custom_fusion.1 = bf16[768,3584]{1,0:T(8,128)(2,1)} fusion(s32[512]{0:T(512)S(1)} %bitcast.95, bf16[512,3584]{1,0:T(8,128)(2,1)} %reshape.258, bf16[]{:T(256)} %constant.17.clone.1), kind=kCustom, calls=%fused_computation.17 | custom fusion | bytes 5505536 | tf_op jit(solution)/shard_map/scatter | solution.py:51
  51.0 0.0 all-to-all-done
  51.0 0.0 copy-start.3
  51.0 9.8 %all-to-all-start.1 = ((bf16[32,1,24,3584]{3,2,1,0:T(8,128)(2,1)}), bf16[32,1,24,3584]{3,2,1,0:T(8,128)(2,1)}, u32[]{:S(2)}, u32[]{:S(2)}) async-start(bf16[32,1,24,3584]{3,2,1,0:T(8,128)(2,1)} %bitcast.89), calls=%async_computation.1 | async-start | bytes 11010048 | tf_op jit(solution)/shard_map/all_to_all | solution.py:59
  60.9 0.3 reduce-scatter.4.cloned.1.call-start
  61.2 121.2 %all-to-all-done.1 = bf16[32,1,24,3584]{3,2,1,0:T(8,128)(2,1)} async-done(((bf16[32,1,24,3584]{3,2,1,0:T(8,128)(2,1)}), bf16[32,1,24,3584]{3,2,1,0:T(8,128)(2,1)}, u32[]{:S(2)}, u32[]{:S(2)}) %all-to-all-start.1) | async-done | bytes 5505056 | tf_op jit(solution)/shard_map/all_to_all | solution.py:59
  182.4 0.0 copy-done.3
  182.4 10.8 %fusion.2 = bf16[1024,3584]{0,1:T(8,128)(2,1)} fusion(bf16[32,1,24,3584]{3,2,1,0:T(8,128)(2,1)} %all-to-all-done.1, f32[32,24]{1,0:T(8,128)S(1)} %bitcast.92, bf16[1,1,32,1,24,1024]{5,4,3,2,1,0:T(8,128)(2,1)S(1)} %copy-done.3), kind=kOutput, calls=%fused_computation.8 | convolution fusion | flops 5649072128 | bytes 14420992 | tf_op jit(solution)/shard_map/qlch,qlcd->hld/dot_general | solution.py:89
  193.2 10.0 %copy.51 = bf16[1024,3584]{1,0:T(8,128)(2,1)} copy(bf16[1024,3584]{0,1:T(8,128)(2,1)} %fusion.2) | data formatting | bytes 14680064
  203.2 0.0 copy-start.2
  203.2 0.0 reduce-scatter.4.cloned.1.call-update
  203.2 0.0 all-reduce.2.cloned.1.call-start
  203.3 0.6 copy-done.2
  203.9 0.6 dynamic_slice.3
  204.4 0.6 fusion.26
  205.1 46.9 %reduce-scatter.4.cloned.1.call-done = bf16[128,3584]{1,0:T(8,128)(2,1)} async-done(((bf16[1024,3584]{1,0:T(8,128)(2,1)}), bf16[128,3584]{1,0:T(8,128)(2,1)}) %reduce-scatter.4.cloned.1.call-update) | async-done | bytes 917520
  252.0 1.5 copy.52
  253.5 1.3 bitcast_convert_fusion.1
  254.9 1.8 copy.45
  256.7 1.3 reshape.237
  258.1 4.7 multiply_convert_fusion.1
  262.8 0.0 all-reduce.2.cloned.1.call-update
  262.8 0.0 all-gather.2.cloned.1.call-start
  262.8 1.2 fusion.25
  264.7 1.4 broadcast_multiply_fusion
  266.1 1.8 copy.46
  267.9 1.3 mul.123
  269.3 156.8 %all-reduce.2.cloned.1.call-done = bf16[3,458752]{1,0:T(4,128)(2,1)} async-done(((bf16[3,458752]{1,0:T(4,128)(2,1)}), bf16[3,458752]{1,0:T(4,128)(2,1)}) %all-reduce.2.cloned.1.call-update) | async-done | bytes 2752528 | tf_op jit(solution)/shard_map/psum | solution.py:102
  426.1 4.7 fusion.22
  430.8 0.0 copy-done
  430.8 1.5 add.64
  432.3 1.7 reshape.233
  434.0 0.1 copy-done.1
  434.0 6.7 %fusion.15 = (bf16[1,128,3584]{2,1,0:T(8,128)(2,1)}, f32[1,128,3584]{2,1,0:T(8,128)}, bf16[1,128,3584]{2,1,0:T(8,128)(2,1)}, bf16[1,128,3584]{2,1,0:T(8,128)(2,1)}) fusion(f32[1,128,3584]{2,1,0:T(8,128)S(1)} %reshape.233, bf16[1,128,3584]{2,1,0:T(8,128)(2,1)S(1)} %copy-done.1, f32[1,128,3584]{2,1,0:T(8,128)} %param.15, bf16[1,128,3584]{2,1,0:T(8,128)(2,1)} %param.16), kind=kLoop, calls=%fused_computation.25 | loop fusion | flops 9175040 | bytes 10092544 | tf_op jit(solution)/shard_map/convert_element_type | solution.py:122
  440.7 0.0 all-gather.2.cloned.1.call-update
  440.7 44.3 %all-gather.2.cloned.1.call-done = bf16[1,1024,3584]{2,1,0:T(8,128)(2,1)} async-done(((bf16[1,128,3584]{2,1,0:T(8,128)(2,1)}), bf16[1,1024,3584]{2,1,0:T(8,128)(2,1)}) %all-gather.2.cloned.1.call-update) | async-done | bytes 7340048 | tf_op jit(solution)/shard_map/all_gather | solution.py:79
  485.0 11.8 %fusion.7 = (f32[32,24]{1,0:T(8,128)}, bf16[1,1,32,1,24,1024]{5,4,3,2,1,0:T(8,128)(2,1)}) fusion(bf16[1,1,32,1,24,1024]{5,4,3,2,1,0:T(8,128)(2,1)} %param.14, f32[32,24]{1,0:T(8,128)S(1)} %bitcast.93, bf16[1,1024,3584]{2,1,0:T(8,128)(2,1)} %all-gather.2.cloned.1.call-done, bf16[32,1,24,3584]{3,2,1,0:T(8,128)(2,1)} %all-to-all-done.1), kind=kOutput, calls=%fused_computation.13 | convolution fusion | flops 5641075712 | bytes 15996928 | tf_op jit(solution)/shard_map/qlcd,lhd->qlch/dot_general | solution.py:76
  496.8 9.9 %all-to-all-start.2 = ((f32[32,1,24]{2,1,0:T(1,128)}), f32[32,1,24]{2,1,0:T(1,128)S(1)}, u32[]{:S(2)}, u32[]{:S(2)}) async-start(f32[32,1,24]{2,1,0:T(1,128)} %bitcast.18), calls=%async_computation.2 | async-start | bytes 32768 | tf_op jit(solution)/shard_map/all_to_all | solution.py:85
  506.7 9.7 %all-to-all-done.2 = f32[32,1,24]{2,1,0:T(1,128)S(1)} async-done(((f32[32,1,24]{2,1,0:T(1,128)}), f32[32,1,24]{2,1,0:T(1,128)S(1)}, u32[]{:S(2)}, u32[]{:S(2)}) %all-to-all-start.2) | async-done | bytes 3104 | tf_op jit(solution)/shard_map/all_to_all | solution.py:85
  516.4 0.5 broadcast.132
  516.9 0.7 reduce.7
  517.6 0.1 reshape.227
  517.7 2.3 gather_fusion
  520.0 0.1 reshape.228
  520.1 0.7 copy.48
  (9 shorter events, 0.1 us)
Async XLA Ops:
  18.5 32.5 %all-to-all-start = ((bf16[32,1,24]{2,1,0:T(2,128)(2,1)}), bf16[32,1,24]{2,1,0:T(2,128)(2,1)S(1)}, u32[]{:S(2)}, u32[]{:S(2)}) async-start(bf16[32,1,24]{2,1,0:T(2,128)(2,1)} %reshape.266), calls=%async_computation | async-start | bytes 32768 | tf_op jit(solution)/shard_map/all_to_all | solution.py:66
  51.0 131.3 %copy-start.3 = (bf16[1,1,32,1,24,1024]{5,4,3,2,1,0:T(8,128)(2,1)S(1)}, bf16[1,1,32,1,24,1024]{5,4,3,2,1,0:T(8,128)(2,1)}, u32[]{:S(2)}) copy-start(bf16[1,1,32,1,24,1024]{5,4,3,2,1,0:T(8,128)(2,1)} %param.14) | copy-start | bytes 4718596
  51.0 131.3 %all-to-all-start.1 = ((bf16[32,1,24,3584]{3,2,1,0:T(8,128)(2,1)}), bf16[32,1,24,3584]{3,2,1,0:T(8,128)(2,1)}, u32[]{:S(2)}, u32[]{:S(2)}) async-start(bf16[32,1,24,3584]{3,2,1,0:T(8,128)(2,1)} %bitcast.89), calls=%async_computation.1 | async-start | bytes 11010048 | tf_op jit(solution)/shard_map/all_to_all | solution.py:59
  60.9 191.1 %reduce-scatter.4.cloned.1.call-start = ((), (), s32[]{:S(2)}) async-start(), calls=%async_computation.6 | async-start | bytes 8257536
  203.2 0.7 copy-start.2
  203.2 222.8 %all-reduce.2.cloned.1.call-start = ((), (), s32[]{:S(2)}) async-start(), calls=%async_computation.5 | async-start | bytes 7340032 | tf_op jit(solution)/shard_map/psum | solution.py:102
  262.8 222.2 %all-gather.2.cloned.1.call-start = ((), (), s32[]{:S(2)}) async-start(), calls=%async_computation.4 | async-start | bytes 8257536 | tf_op jit(solution)/shard_map/all_gather | solution.py:79
  269.3 161.6 %copy-start = (f32[458752]{0:T(1024)S(1)}, f32[458752]{0:T(1024)}, u32[]{:S(2)}) copy-start(f32[458752]{0:T(1024)} %mul.123) | copy-start | bytes 5505028
  432.3 1.7 copy-start.1
  496.8 19.6 %all-to-all-start.2 = ((f32[32,1,24]{2,1,0:T(1,128)}), f32[32,1,24]{2,1,0:T(1,128)S(1)}, u32[]{:S(2)}, u32[]{:S(2)}) async-start(f32[32,1,24]{2,1,0:T(1,128)} %bitcast.18), calls=%async_computation.2 | async-start | bytes 32768 | tf_op jit(solution)/shard_map/all_to_all | solution.py:85
Sparse Core Ops, SparseCore 0:
  203.4 48.5 reduce-scatter.3
  262.9 163.1 all-reduce.1
  440.8 44.1 all-gather.1
where the time goes:
time: 529 us; the launch traced here: 527 us
  waiting for transfers between devices  379 us (72%)
  local copies, waits for them, and re-layouts  52 us (10%)
  starting transfers between devices  31.7 us (6%)
  matrix products  27.3 us (5%)
  other arithmetic  22.7 us (4%)
  between operations  14.6 us (3%)
    psum x1, waiting for transfers between devices, on_device(): lax.psum(grad_table.astype(jnp.bfloat16), 'expert').astype(jnp.float32)  157 us
    all_to_all x1, waiting for transfers between devices, on_device(): lax.all_to_all(send_rows.reshape(dev_count, slot_dev, capacity, feature_c...  121 us
    unnamed x4, waiting for transfers between devices  46.9 us
    all_gather x1, waiting for transfers between devices, on_device(): lax.all_gather(weights, 'dp', axis=1, tiled=True)  44.3 us
    unnamed x13, local copies, waits for them, and re-layouts  14.4 us
    dot_general x1, matrix products, on_device(): jnp.einsum('qlcd,lhd->qlch', recv_rows, lax.all_gather(weights, 'dp', axi...  11.8 us
    all_to_all x1, starting transfers between devices, on_device(): lax.all_to_all(send_gates.reshape(dev_count, slot_dev, capacity), 'expert...  11.7 us
    dot_general x1, matrix products, on_device(): jnp.einsum('qlch,qlcd->hld', hidden, scaled, preferred_element_type=jnp.f...  10.8 us
  transfers between devices with their start and end apart: 6, of which 5 were waited for; matrix products, arithmetic and copies ran while one was open for 5% of the time, Pallas kernels for 0%

commit v1 on v0

v1 whole, which is shorter than its diff:
```python
import jax
import jax.numpy as jnp
from jax import lax
from jax.sharding import PartitionSpec as P

beta_one = 0.9
beta_two = 0.95
learn_rate = 0.00022
decay_rate = 0.1
epsilon = 1e-08
correct_one = 0.6513215599
correct_two = 0.4012630607


def on_device(
    grad_out,
    gate_probs,
    expert_route,
    replica_pick,
    slot_expert,
    saved_hidden,
    master,
    first_moment,
    second_moment,
):
    slots = slot_expert.shape[0]
    cap = saved_hidden.shape[4]
    feats = grad_out.shape[1]
    toks, top = gate_probs.shape
    rows_own = master.shape[1]
    weights = lax.optimization_barrier(master[0].astype(jnp.bfloat16))
    gathered = lax.all_gather(weights, "dp", axis=0, tiled=True)
    ids = jnp.arange(slots, dtype=jnp.int32)
    same = slot_expert[:, None] == slot_expert[None, :]
    rank = jnp.sum(same & (ids[None, :] < ids[:, None]), axis=1)
    route = expert_route.T[:, None, :]
    pick = replica_pick.T
    host = slot_expert[None, :, None] == route
    copies = jnp.sum(host.astype(jnp.int32), axis=1)
    chosen = host & (rank[None, :, None] == (pick % copies)[:, None, :])
    taken = jnp.any(chosen, axis=0)
    order = jnp.arange(toks, dtype=jnp.int32)
    before = (order[:, None] < order[None, :]).astype(jnp.bfloat16)
    place = jnp.dot(taken.astype(jnp.bfloat16), before, preferred_element_type=jnp.float32)
    gate_of = jnp.sum(
        jnp.where(chosen, gate_probs.T.astype(jnp.bfloat16).astype(jnp.float32)[:, None, :], 0.0), axis=0
    )
    spot = jnp.where(taken, place.astype(jnp.int32), -1)
    hot = spot[:, None, :] == jnp.arange(cap, dtype=jnp.int32)[None, :, None]
    send_gates = jnp.sum(jnp.where(hot, gate_of[:, None, :], 0.0), axis=2).astype(jnp.bfloat16)
    send_rows = jnp.dot(
        hot.astype(jnp.bfloat16).reshape(slots * cap, toks), grad_out, preferred_element_type=jnp.float32
    ).astype(jnp.bfloat16)
    rows = lax.all_to_all(
        send_rows.reshape(slots, cap, feats), "expert", split_axis=0, concat_axis=0, tiled=True
    ).reshape(slots * cap, feats)
    gates = lax.all_to_all(send_gates, "expert", split_axis=0, concat_axis=0, tiled=True)
    scale = gates.astype(jnp.float32).reshape(slots * cap, 1)
    hidden = saved_hidden.reshape(slots * cap, -1)
    gated = (hidden.astype(jnp.float32) * scale).astype(jnp.bfloat16)
    partial = lax.dot_general(
        gated, rows, (((0,), (0,)), ((), ())), preferred_element_type=jnp.float32
    ).astype(jnp.bfloat16)
    reduced = lax.psum_scatter(partial, "dp", scatter_dimension=0, tiled=True)
    projected = lax.dot_general(rows, gathered, (((1,), (1,)), ((), ())), preferred_element_type=jnp.float32)
    hidden_grad = (scale * projected).astype(jnp.bfloat16).reshape(saved_hidden.shape)
    terms = jnp.sum(hidden.astype(jnp.float32) * projected, axis=-1).reshape(slots, cap)
    returned = lax.all_to_all(terms, "expert", split_axis=0, concat_axis=0, tiled=True)
    by_token = jnp.sum(jnp.where(hot, returned[:, :, None], 0.0), axis=1)
    gate_grad = jnp.sum(jnp.where(chosen, by_token[None], 0.0), axis=1).T
    part = rows_own // slots
    shards = lax.all_to_all(
        reduced.reshape(slots, part, feats), "expert", split_axis=0, concat_axis=0, tiled=True
    )
    summed = lax.dot_general(
        same.astype(jnp.bfloat16),
        shards,
        (((1,), (0,)), ((), ())),
        preferred_element_type=jnp.float32,
    ).astype(jnp.bfloat16)
    back = lax.all_to_all(summed, "expert", split_axis=0, concat_axis=0, tiled=True)
    total = back.reshape(1, rows_own, feats).astype(jnp.float32)
    new_first = beta_one * first_moment.astype(jnp.float32) + (1.0 - beta_one) * total
    new_second = beta_two * second_moment.astype(jnp.float32) + (1.0 - beta_two) * total * total
    update = (
        new_first / correct_one / (jnp.sqrt(new_second / correct_two) + epsilon) + decay_rate * master
    )
    new_master = master - learn_rate * update
    return (
        hidden_grad,
        gate_grad,
        new_master,
        new_first.astype(jnp.bfloat16),
        new_second.astype(jnp.bfloat16),
    )


def solution(mesh):
    tokens = P(("dp", "expert"), None)
    acts = P("dp", "expert", None, None, None, None)
    shard = P("expert", "dp", None)
    return jax.shard_map(
        on_device,
        mesh=mesh,
        in_specs=(tokens, tokens, tokens, tokens, P(), acts, shard, shard, shard),
        out_specs=(acts, tokens, shard, shard, shard),
        check_vma=False,
    )
```

time: 529 us -> 334 us (0.63)
  waiting for transfers between devices: 379 us -> 194 us
  blocking collectives: 0 us -> 49 us
  local copies, waits for them, and re-layouts: 52 us -> 7.07 us
  other arithmetic: 22.7 us -> 14 us
    psum x1 -> x0, waiting for transfers between devices: 157 us -> none  [on_device(): lax.psum(grad_table.astype(jnp.bfloat16), 'expert').astype(jnp.float32)]
    all_to_all x0 -> x2, blocking collectives: none -> 49 us  [the longest x1 36.3 us: on_device(): lax.all_to_all(reduced.reshape(slots, part, feats), 'expert', split_axis=...]
    unnamed x4 -> x2, waiting for transfers between devices: 46.9 us -> 0.03 us
    all_gather x1, waiting for transfers between devices: 44.3 us -> 0.01 us  [on_device(): gathered = lax.all_gather(weights, 'dp', axis=0, tiled=True)]
    reduce_scatter x0 -> x1, waiting for transfers between devices: none -> 42.2 us  [on_device(): reduced = lax.psum_scatter(partial, 'dp', scatter_dimension=0, tiled=True)]
    all_to_all x3, waiting for transfers between devices: 131 us -> 152 us  [the longest x1 121 us: on_device(): lax.all_to_all(send_rows.reshape(slots, cap, feats), 'expert', split_axis...]
    unnamed x13 -> x14, local copies, waits for them, and re-layouts: 14.4 us -> 0.03 us
    scatter x2 -> x0, local copies, waits for them, and re-layouts: 14 us -> none  [the longest x1 10.2 us: on_device(): jnp.zeros((slot_count * capacity, feature_count), jnp.bfloat16)]
  transfers between devices with their start and end apart: 6 -> 5, of which waited for: 5 -> 4; matrix products, arithmetic and copies ran while one was open for 5% -> 3% of each run, Pallas kernels for 0% -> 0%
where the time goes in v1:
time: 334 us
  waiting for transfers between devices  194 us (58%)
  blocking collectives  49 us (15%)
  starting transfers between devices  29.5 us (9%)
  matrix products  26.1 us (8%)
  between operations  14.2 us (4%)
  other arithmetic  14 us (4%)
  local copies, waits for them, and re-layouts  7.07 us (2%)
    all_to_all x1, waiting for transfers between devices, on_device(): lax.all_to_all(send_rows.reshape(slots, cap, feats), 'expert', split_axis...  121 us
    reduce_scatter x1, waiting for transfers between devices, on_device(): reduced = lax.psum_scatter(partial, 'dp', scatter_dimension=0, tiled=True)  42.2 us
    all_to_all x1, blocking collectives, on_device(): lax.all_to_all(reduced.reshape(slots, part, feats), 'expert', split_axis=...  36.3 us
    all_to_all x1, waiting for transfers between devices, on_device(): lax.all_to_all(summed, 'expert', split_axis=0, concat_axis=0, tiled=True)  20.9 us
    all_to_all x1, blocking collectives, on_device(): lax.all_to_all(send_gates, 'expert', split_axis=0, concat_axis=0, tiled=T...  12.7 us
    all_to_all x1, starting transfers between devices, on_device(): lax.all_to_all(send_rows.reshape(slots, cap, feats), 'expert', split_axis...  11.7 us
    all_to_all x1, starting transfers between devices, on_device(): lax.all_to_all(terms, 'expert', split_axis=0, concat_axis=0, tiled=True)  11.6 us
    dot_general x1, matrix products, on_device(): lax.dot_general(rows, gathered, (((1,), (1,)), ((), ())), preferred_eleme...  11 us
  transfers between devices with their start and end apart: 5, of which 4 were waited for; matrix products, arithmetic and copies ran while one was open for 3% of the time, Pallas kernels for 0%

profile of v1, /device:TPU:2, one launch (start us, length us, event | category | flops | bytes accessed | tf_op | source)
XLA Modules:
  0.0 333.9 jit_solution(12791349967939616283)
XLA Ops:
  7.2 0.0 copy-start
  7.2 0.0 copy-start.4
  7.2 0.0 copy-start.3
  7.2 0.0 copy-start.5
  7.2 0.0 all-gather.2.cloned.1.call-start
  7.3 2.6 convert_bitcast_fusion
  9.8 0.0 all-gather.2.cloned.1.call-update
  9.9 0.1 eq.82
  10.0 0.0 copy-done.4
  10.0 0.2 convert_reduce_fusion
  10.1 0.0 copy-done.3
  10.2 0.1 fusion.6
  10.2 0.0 copy-done.5
  10.3 0.1 add_select_fusion
  10.4 0.1 fusion.7
  10.5 0.1 fusion.2
  10.6 0.2 bitcast_compare_fusion
  10.8 0.0 copy-done
  10.8 3.9 %convolution_convert_fusion.1 = bf16[768,3584]{1,0:T(8,128)(2,1)} fusion(pred[768,128]{1,0:T(32,128)(4,1)S(1)} %bitcast_compare_fusion, bf16[128,3584]{1,0:T(8,128)(2,1)S(1)} %copy-done), kind=kOutput, calls=%fused_computation.1 | convolution fusion | flops 707395584 | bytes 6520832 | tf_op jit(solution)/shard_map/dot_general | solution.py:51
  14.7 0.0 copy-start.6
  14.7 0.0 copy-start.2
  14.7 11.7 %all-to-all-start.1 = ((bf16[32,24,3584]{2,1,0:T(8,128)(2,1)}), bf16[32,24,3584]{2,1,0:T(8,128)(2,1)}, u32[]{:S(2)}, u32[]{:S(2)}) async-start(bf16[32,24,3584]{2,1,0:T(8,128)(2,1)} %bitcast.38), calls=%async_computation.1 | async-start | bytes 11010048 | tf_op jit(solution)/shard_map/all_to_all | solution.py:54
  26.5 0.0 copy-done.6
  26.5 121.5 %all-to-all-done.1 = bf16[32,24,3584]{2,1,0:T(8,128)(2,1)} async-done(((bf16[32,24,3584]{2,1,0:T(8,128)(2,1)}), bf16[32,24,3584]{2,1,0:T(8,128)(2,1)}, u32[]{:S(2)}, u32[]{:S(2)}) %all-to-all-start.1) | async-done | bytes 5505056 | tf_op jit(solution)/shard_map/all_to_all | solution.py:54
  148.0 0.0 all-gather.2.cloned.1.call-done
  148.0 0.0 copy-done.2
  148.0 11.0 %fusion = (f32[768]{0:T(1024)S(1)}, f32[768,1024]{1,0:T(8,128)}) fusion(bf16[1,1,32,1,24,1024]{5,4,3,2,1,0:T(8,128)(2,1)S(1)} %copy-done.2, bf16[768,3584]{1,0:T(8,128)(2,1)} %bitcast.6, bf16[1024,3584]{1,0:T(8,128)(2,1)} %all-gather.2.cloned.1.call-done), kind=kOutput, calls=%fused_computation.4 | convolution fusion | flops 5639502848 | bytes 17566720 | tf_op jit(solution)/shard_map/dot_general | solution.py:65
  159.0 0.7 all_to_all.21
  159.7 11.6 %all-to-all-start.2 = ((f32[32,1,24]{2,1,0:T(1,128)}), f32[32,1,24]{2,1,0:T(1,128)S(1)}, u32[]{:S(2)}, u32[]{:S(2)}) async-start(f32[32,1,24]{2,1,0:T(1,128)} %bitcast.11), calls=%async_computation.2 | async-start | bytes 32768 | tf_op jit(solution)/shard_map/all_to_all | solution.py:68
  171.3 0.0 reduce-scatter.2.cloned.1.call-start
  171.4 0.1 select_reduce_fusion.3
  171.4 9.5 %all-to-all-done.2 = f32[32,1,24]{2,1,0:T(1,128)S(1)} async-done(((f32[32,1,24]{2,1,0:T(1,128)}), f32[32,1,24]{2,1,0:T(1,128)S(1)}, u32[]{:S(2)}, u32[]{:S(2)}) %all-to-all-start.2) | async-done | bytes 3104 | tf_op jit(solution)/shard_map/all_to_all | solution.py:68
  181.0 0.3 select_reduce_fusion
  181.3 0.1 copy.34
  181.4 0.1 copy.35
  181.5 12.7 %all_to_all.30 = bf16[32,1,24]{2,1,0:T(2,128)(2,1)S(1)} all-to-all(bf16[32,1,24]{2,1,0:T(2,128)(2,1)S(1)} %copy.35), channel_id=1, replica_groups=mesh['dp'=8,'expert'=32] {'expert'}, dimensions={0} | all-to-all | bytes 3072 | tf_op jit(solution)/shard_map/all_to_all | solution.py:57
  194.2 0.3 multiply_convert_fusion
  194.5 10.5 %convolution_convert_fusion = bf16[1024,3584]{1,0:T(8,128)(2,1)} fusion(bf16[768,1024]{1,0:T(8,128)(2,1)S(1)} %bitcast.39, bf16[768,3584]{1,0:T(8,128)(2,1)} %bitcast.6), kind=kOutput, calls=%fused_computation | convolution fusion | flops 5640814592 | bytes 14417920 | tf_op jit(solution)/shard_map/dot_general | solution.py:61
  205.1 0.0 reduce-scatter.2.cloned.1.call-update
  205.1 42.2 %reduce-scatter.2.cloned.1.call-done = bf16[128,3584]{1,0:T(8,128)(2,1)} async-done(((bf16[1024,3584]{1,0:T(8,128)(2,1)}), bf16[128,3584]{1,0:T(8,128)(2,1)}) %reduce-scatter.2.cloned.1.call-update) | async-done | bytes 917520 | tf_op jit(solution)/shard_map/reduce_scatter | solution.py:64
  247.3 1.8 reshape.108
  249.1 36.3 %all_to_all.31 = bf16[32,4,3584]{2,1,0:T(4,128)(2,1)S(1)} all-to-all(bf16[32,4,3584]{2,1,0:T(4,128)(2,1)S(1)} %reshape.108), channel_id=1, replica_groups=mesh['dp'=8,'expert'=32] {'expert'}, dimensions={0} | all-to-all | bytes 1835008 | tf_op jit(solution)/shard_map/all_to_all | solution.py:72
  285.4 0.5 convolution_convert_fusion.2
  285.9 1.6 copy.38
  287.5 6.0 %all-to-all-start.4 = ((bf16[32,4,3584]{2,1,0:T(4,128)(2,1)}), bf16[32,4,3584]{2,1,0:T(4,128)(2,1)}, u32[]{:S(2)}, u32[]{:S(2)}) async-start(bf16[32,4,3584]{2,1,0:T(4,128)(2,1)} %copy.38), calls=%async_computation.5 | async-start | bytes 1835008 | tf_op jit(solution)/shard_map/all_to_all | solution.py:81
  293.5 0.7 select_reduce_fusion.2
  294.2 0.1 convert_reduce_fusion.1
  294.3 0.1 reshape.109
  294.3 3.3 multiply_convert_fusion.1
  297.6 0.0 copy-start.1
  297.6 20.9 %all-to-all-done.4 = bf16[32,4,3584]{2,1,0:T(4,128)(2,1)} async-done(((bf16[32,4,3584]{2,1,0:T(4,128)(2,1)}), bf16[32,4,3584]{2,1,0:T(4,128)(2,1)}, u32[]{:S(2)}, u32[]{:S(2)}) %all-to-all-start.4) | async-done | bytes 917536 | tf_op jit(solution)/shard_map/all_to_all | solution.py:81
  318.5 2.6 reshape.112
  321.1 0.0 copy-done.1
  321.1 6.0 %fusion.4 = (bf16[1,128,3584]{2,1,0:T(8,128)(2,1)}, f32[1,128,3584]{2,1,0:T(8,128)}, bf16[1,128,3584]{2,1,0:T(8,128)(2,1)}) fusion(f32[1,128,3584]{2,1,0:T(8,128)} %reshape.112, bf16[1,128,3584]{2,1,0:T(8,128)(2,1)} %param.17, f32[1,128,3584]{2,1,0:T(8,128)S(1)} %copy-done.1, bf16[1,128,3584]{2,1,0:T(8,128)(2,1)} %param.16), kind=kLoop, calls=%fused_computation.14 | loop fusion | flops 8716288 | bytes 9175040 | tf_op jit(solution)/shard_map/convert_element_type | solution.py:94
  (3 shorter events, 0.0 us)
Async XLA Ops:
  7.2 3.6 %copy-start = (bf16[128,3584]{1,0:T(8,128)(2,1)S(1)}, bf16[128,3584]{1,0:T(8,128)(2,1)}, u32[]{:S(2)}) copy-start(bf16[128,3584]{1,0:T(8,128)(2,1)} %param.9) | copy-start | bytes 2752516
  7.2 2.8 copy-start.4
  7.2 3.0 copy-start.3
  7.2 3.0 copy-start.5
  7.2 140.8 %all-gather.2.cloned.1.call-start = ((), (), s32[]{:S(2)}) async-start(), calls=%async_computation.6 | async-start | bytes 8257536 | tf_op jit(solution)/shard_map/all_gather | solution.py:32
  14.7 11.7 %copy-start.6 = (f32[128,4]{0,1:T(4,128)S(1)}, f32[128,4]{0,1:T(4,128)}, u32[]{:S(2)}) copy-start(f32[128,4]{0,1:T(4,128)} %param.10) | copy-start | bytes 6148
  14.7 133.3 %copy-start.2 = (bf16[1,1,32,1,24,1024]{5,4,3,2,1,0:T(8,128)(2,1)S(1)}, bf16[1,1,32,1,24,1024]{5,4,3,2,1,0:T(8,128)(2,1)}, u32[]{:S(2)}) copy-start(bf16[1,1,32,1,24,1024]{5,4,3,2,1,0:T(8,128)(2,1)} %param.14) | copy-start | bytes 4718596
  14.7 133.2 %all-to-all-start.1 = ((bf16[32,24,3584]{2,1,0:T(8,128)(2,1)}), bf16[32,24,3584]{2,1,0:T(8,128)(2,1)}, u32[]{:S(2)}, u32[]{:S(2)}) async-start(bf16[32,24,3584]{2,1,0:T(8,128)(2,1)} %bitcast.38), calls=%async_computation.1 | async-start | bytes 11010048 | tf_op jit(solution)/shard_map/all_to_all | solution.py:54
  159.7 21.3 %all-to-all-start.2 = ((f32[32,1,24]{2,1,0:T(1,128)}), f32[32,1,24]{2,1,0:T(1,128)S(1)}, u32[]{:S(2)}, u32[]{:S(2)}) async-start(f32[32,1,24]{2,1,0:T(1,128)} %bitcast.11), calls=%async_computation.2 | async-start | bytes 32768 | tf_op jit(solution)/shard_map/all_to_all | solution.py:68
  171.3 76.0 %reduce-scatter.2.cloned.1.call-start = ((), (), s32[]{:S(2)}) async-start(), calls=%async_computation.7 | async-start | bytes 8257536 | tf_op jit(solution)/shard_map/reduce_scatter | solution.py:64
  287.5 31.0 %all-to-all-start.4 = ((bf16[32,4,3584]{2,1,0:T(4,128)(2,1)}), bf16[32,4,3584]{2,1,0:T(4,128)(2,1)}, u32[]{:S(2)}, u32[]{:S(2)}) async-start(bf16[32,4,3584]{2,1,0:T(4,128)(2,1)} %copy.38), calls=%async_computation.5 | async-start | bytes 1835008 | tf_op jit(solution)/shard_map/all_to_all | solution.py:81
  297.6 23.4 %copy-start.1 = (f32[1,128,3584]{2,1,0:T(8,128)S(1)}, f32[1,128,3584]{2,1,0:T(8,128)}, u32[]{:S(2)}) copy-start(f32[1,128,3584]{2,1,0:T(8,128)} %param.15) | copy-start | bytes 5505028
Sparse Core Ops, SparseCore 0:
  10.5 49.9 all-gather.1
  205.2 42.0 reduce-scatter.1

commit v2 on v1

v2 whole, which is shorter than its diff:
```python
import functools

import jax
import jax.numpy as jnp
from jax import lax
from jax.experimental import pallas as pl
from jax.experimental.pallas import tpu as pltpu
from jax.sharding import PartitionSpec as P

HOT = 3
CORES = 2
BF = jnp.bfloat16
F32 = jnp.float32
MESH = pl.DeviceIdType.MESH

beta_one = 0.9
beta_two = 0.95
learn_rate = 0.00022
decay_rate = 0.1
epsilon = 1e-08
correct_one = 0.6513215599
correct_two = 0.4012630607


def kernel(
    nx,
    ny,
    nz,
    chunks,
    cap,
    meta,
    share,
    tok,
    hid,
    mas,
    fst,
    snd,
    hg,
    back,
    nm,
    nf,
    ns,
    xg,
    wg,
    sendy,
    rows,
    pick2,
    gcol,
    gated,
    proj,
    csend,
    crecv,
    ownh,
    xsend,
    xrecv,
    xown,
    gsh,
    hs1,
    hr1,
    ts,
    tr,
    hs2,
    hr2,
    mz,
    rel,
    relr,
    ret,
    retr,
    bz,
    bk,
    load_sem,
    zs,
    zr,
    ys,
    yr,
    wxs,
    wxr,
    wcs,
    wcr,
    cs,
    cr,
    xs,
    xr,
    h1s,
    h1r,
    tss,
    tsr,
    h2s,
    h2r,
    ms,
    mr,
    rs,
    rr,
    qs,
    qr,
    bs,
    br,
):
    p, q = lax.axis_index("dp"), lax.axis_index("expert")
    x, c = p // CORES, lax.rem(p, CORES)
    z, y = q // ny, lax.rem(q, ny)
    toks = xg.shape[2]
    dk = xg.shape[3]
    shard = wg.shape[3]
    far, near = nz // 2, nz - 1 - nz // 2
    block = nz * cap
    pair = 2 * cap
    part = shard // nz

    def at_x(j):
        return lax.rem(x + j + nx, nx)

    def at_y(j):
        return lax.rem(y + j + ny, ny)

    def at_z(j):
        return lax.rem(z + j + nz, nz)

    def remote(src, dst, ssem, rsem, pp, qq):
        return pltpu.make_async_remote_copy(
            src_ref=src, dst_ref=dst, send_sem=ssem, recv_sem=rsem, device_id=(pp, qq), device_id_type=MESH
        )

    def lanes(k):
        return pl.ds(pl.multiple_of(k * dk, 128), dk)

    def load(k):
        return pltpu.make_async_copy(tok.at[:, lanes(k)], xg.at[k, z], load_sem.at[k])

    for k in range(chunks):
        load(k).start()

    barrier = pltpu.get_barrier_semaphore()
    peers = [(p, at_z(j) * ny + y) for j in range(1, nz)]
    peers += [(p, z * ny + at_y(j)) for j in range(1, ny)]
    peers += [(at_x(j) * CORES + c, q) for j in range(1, nx)]
    other = x * CORES + 1 - c
    peers += [(other, q)]
    for peer in peers:
        pl.semaphore_signal(barrier, inc=1, device_id=peer, device_id_type=MESH)
    pl.semaphore_wait(barrier, len(peers))

    def meta_copy(j):
        return remote(meta.at[at_z(j)], mz.at[z], ms.at[j - 1], mr.at[j - 1], p, at_z(j) * ny + y)

    def rel_copy(j):
        return remote(rel.at[at_y(j)], relr.at[y], rs.at[j - 1], rr.at[j - 1], p, z * ny + at_y(j))

    def ret_copy(j):
        return remote(ret.at[at_y(j)], retr.at[y], qs.at[j - 1], qr.at[j - 1], p, z * ny + at_y(j))

    def back_copy(j):
        return remote(bz.at[at_z(j)], bk.at[z], bs.at[j - 1], br.at[j - 1], p, at_z(j) * ny + y)

    def hop(d, h, k):
        sign = 1 - 2 * d
        origin = lax.rem(z - sign * (h - 1) + nz, nz)
        to = lax.rem(z + sign + nz, nz)
        return remote(
            xg.at[k, origin], xg.at[k, origin], zs.at[d, h - 1, k], zr.at[d, h - 1, k], p, to * ny + y
        )

    def hops(h, k):
        if h <= near:
            return [hop(0, h, k), hop(1, h, k)]
        if h <= far:
            return [hop(lax.rem(k, 2), h, k)]
        return []

    def weight_copy(j, k):
        return remote(
            wg.at[k, c, x], wg.at[k, c, x], wxs.at[j - 1, k], wxr.at[j - 1, k], at_x(j) * CORES + c, q
        )

    def weight_pass(k):
        return remote(wg.at[k, c], wg.at[k, c], wcs.at[k], wcr.at[k], other, q)

    def row_copy(j, k):
        return remote(
            sendy.at[lax.rem(k, 2), at_y(j)],
            rows.at[k, y],
            ys.at[j - 1, k],
            yr.at[j - 1, k],
            p,
            z * ny + at_y(j),
        )

    def core_copy(k):
        return remote(csend.at[lax.rem(k, 2)], crecv.at[k], cs.at[k], cr.at[k], other, q)

    def x_copy(j, k):
        return remote(
            xsend.at[lax.rem(k, 2), at_x(j)],
            xrecv.at[k, x],
            xs.at[j - 1, k],
            xr.at[j - 1, k],
            at_x(j) * CORES + c,
            q,
        )

    def first_copy(j, k):
        return remote(
            hs1.at[k, at_z(j)], hr1.at[k, z], h1s.at[j - 1, k], h1r.at[j - 1, k], p, at_z(j) * ny + y
        )

    def table_copy(j, k):
        return remote(ts.at[k], tr.at[k, y], tss.at[j - 1, k], tsr.at[j - 1, k], p, z * ny + at_y(j))

    def second_copy(j, k):
        return remote(
            hs2.at[k, at_z(j)], hr2.at[k, z], h2s.at[j - 1, k], h2r.at[j - 1, k], p, at_z(j) * ny + y
        )

    def when(k):
        return pl.when((k >= 0) & (k < chunks))

    for j in range(1, nz):
        meta_copy(j).start()
    mz[z] = meta[z]
    proj[...] = jnp.zeros_like(proj)

    spot_row = lax.broadcasted_iota(jnp.int32, (cap, toks), 0).astype(F32)

    def step(tau, carry):
        for h in range(far, 0, -1):

            @when(tau - h)
            def _(h=h, k=tau - h):
                for copy in hops(h, k):
                    copy.wait()
                for copy in hops(h + 1, k):
                    copy.start()

        @when(tau)
        def _(k=tau):
            load(k).wait()
            for copy in hops(1, k):
                copy.start()
            wg[k, c, x] = mas[:, lanes(k)].astype(BF)
            for j in range(1, nx):
                weight_copy(j, k).start()

        @when(tau - 2)
        def _(k=tau - 2):
            for j in range(1, nx):
                weight_copy(j, k).wait()
            weight_pass(k).start()

        @pl.when(tau == 1)
        def _():
            for j in range(1, nz):
                meta_copy(j).wait()
            for yy in range(ny):
                for zz in range(nz):
                    rel[yy, zz : zz + 1, :] = mz[zz, yy : yy + 1, :]
                    rel[yy, nz + zz : nz + zz + 1, :] = mz[zz, ny + yy : ny + yy + 1, :]
            for j in range(1, ny):
                rel_copy(j).start()
            relr[y] = rel[y]
            zero = jnp.zeros((cap, toks), F32)
            for jj in range(nz // 2):
                for yy in range(ny):
                    one = [
                        jnp.where(mz[2 * jj + i, yy : yy + 1, :] == spot_row, 1.0, 0.0) for i in (0, 1)
                    ]
                    top = jnp.concatenate([one[0], zero], axis=1)
                    low = jnp.concatenate([zero, one[1]], axis=1)
                    pick2[jj, yy * pair : (yy + 1) * pair, :] = jnp.concatenate([top, low], axis=0).astype(BF)

        @pl.when(tau == 2)
        def _():
            for j in range(1, ny):
                rel_copy(j).wait()
            for yy in range(ny):
                for zz in range(nz):
                    hit = relr[yy, zz : zz + 1, :] == spot_row
                    gate = jnp.where(hit, relr[yy, nz + zz : nz + zz + 1, :], 0.0)
                    column = jnp.sum(gate, axis=1, keepdims=True)
                    start = yy * block + zz * cap
                    gcol[start : start + cap, :] = jnp.broadcast_to(column, (cap, 128))

            def turn(i, carry):
                here = pl.ds(pl.multiple_of(i * 128, 128), 128)
                scaled = hid[here, :].astype(F32) * gcol[here, :][:, 0:1]
                gated[:, here] = scaled.T.astype(BF)
                return carry

            lax.fori_loop(0, hid.shape[0] // 128, turn, 0)

        @when(tau - far)
        def _(k=tau - far):
            slot = lax.rem(k, 2)

            def choose(jj, carry):
                two = xg[k, pl.ds(2 * jj, 2)].reshape(2 * toks, dk)
                got = jnp.dot(pick2[jj], two, preferred_element_type=F32).astype(BF)
                here = pl.ds(pl.multiple_of(jj * pair, pair), pair)
                for yy in range(ny):
                    sendy[slot, yy, here, :] = got[yy * pair : (yy + 1) * pair, :]
                return carry

            lax.fori_loop(0, nz // 2, choose, 0)
            for j in range(1, ny):
                row_copy(j, k).start()
            rows[k, y] = sendy[slot, y]

        @when(tau - far - 6)
        def _(k=tau - far - 6):
            for j in range(1, nz):
                second_copy(j, k).wait()
            flag = share[0, q]
            for e in range(1, HOT):
                flag = flag + share[e, q]

            def adam(b, carry):
                here = pl.ds(pl.multiple_of(b * part, part), part)
                grad = flag * hr2[k, b].astype(F32) + (1.0 - flag) * gsh[k, here, :]
                old = mas[here, lanes(k)]
                first = beta_one * fst[here, lanes(k)].astype(F32) + (1.0 - beta_one) * grad
                second = beta_two * snd[here, lanes(k)].astype(F32) + (1.0 - beta_two) * grad * grad
                update = first / correct_one / (jnp.sqrt(second / correct_two) + epsilon) + decay_rate * old
                nm[here, lanes(k)] = old - learn_rate * update
                nf[here, lanes(k)] = first.astype(BF)
                ns[here, lanes(k)] = second.astype(BF)
                return carry

            lax.fori_loop(0, nz, adam, 0)

        @when(tau - far - 5)
        def _(k=tau - far - 5):
            for j in range(1, ny):
                table_copy(j, k).wait()
            total = []
            for e in range(HOT):
                acc = tr[k, 0, e].astype(F32)
                for yy in range(1, ny):
                    acc = acc + tr[k, yy, e].astype(F32)
                total.append(acc)
            for zz in range(nz):
                acc = share[0, zz * ny + y] * total[0]
                for e in range(1, HOT):
                    acc = acc + share[e, zz * ny + y] * total[e]
                hs2[k, zz] = acc.astype(BF)
            for j in range(1, nz):
                second_copy(j, k).start()
            hr2[k, z] = hs2[k, z]

        @when(tau - far - 4)
        def _(k=tau - far - 4):
            for j in range(1, nz):
                first_copy(j, k).wait()
            sums = [jnp.zeros((part, dk), F32)] * HOT
            for zz in range(nz):
                value = hr1[k, zz].astype(F32)
                sums = [sums[e] + share[e, zz * ny + y] * value for e in range(HOT)]
            for e in range(HOT):
                ts[k, e] = sums[e].astype(BF)
            for j in range(1, ny):
                table_copy(j, k).start()
            tr[k, y] = ts[k]

        @when(tau - far - 3)
        def _(k=tau - far - 3):
            for j in range(1, nx):
                x_copy(j, k).wait()

            def add(b, carry):
                here = pl.ds(pl.multiple_of(b * part, part), part)
                value = xown[here, :]
                for j in range(1, nx):
                    value = value + xrecv[k, at_x(-j), here, :].astype(F32)
                gsh[k, here, :] = value
                hs1[k, b] = value.astype(BF)
                return carry

            lax.fori_loop(0, nz, add, 0)
            for j in range(1, nz):
                first_copy(j, k).start()
            hr1[k, z] = hs1[k, z]

        @when(tau - far - 2)
        def _(k=tau - far - 2):
            core_copy(k).wait()
            for j in range(1, nx):
                xsend[lax.rem(k, 2), at_x(j)] = (ownh[at_x(j)] + crecv[k, at_x(j)].astype(F32)).astype(BF)
                x_copy(j, k).start()
            xown[...] = ownh[x] + crecv[k, x].astype(F32)

        @when(tau - far - 1)
        def _(k=tau - far - 1):
            for j in range(1, ny):
                row_copy(j, k).wait()
            slot = lax.rem(k, 2)

            def half(xx, core):
                here = pl.ds(pl.multiple_of((xx * CORES + core) * shard, shard), shard)
                return jnp.dot(
                    gated[here, :], rows[k].reshape(ny * block, dk), preferred_element_type=F32
                )

            def theirs(xx, carry):
                csend[slot, xx] = half(xx, 1 - c).astype(BF)
                return carry

            def mine(xx, carry):
                ownh[xx] = half(xx, c)
                return carry

            def project(xx, carry):
                w = jnp.concatenate([wg[k, 0, xx], wg[k, 1, xx]], axis=0)
                here = pl.ds(pl.multiple_of(xx * CORES * shard, CORES * shard), CORES * shard)
                proj[:, here] += lax.dot_general(
                    rows[k].reshape(ny * block, dk), w, (((1,), (1,)), ((), ())), preferred_element_type=F32
                )
                return carry

            lax.fori_loop(0, nx, theirs, 0)
            core_copy(k).start()
            lax.fori_loop(0, nx, mine, 0)
            weight_pass(k).wait()
            lax.fori_loop(0, nx, project, 0)

        @pl.when(tau == chunks + far + 1)
        def _():
            def finish(i, carry):
                yy, jj = i // (nz // 2), lax.rem(i, nz // 2)
                here = pl.ds(pl.multiple_of(i * pair, pair), pair)
                value = proj[here, :]
                hg[here, :] = (gcol[here, :][:, 0:1] * value).astype(BF)
                term = jnp.sum(hid[here, :].astype(F32) * value, axis=1, keepdims=True)
                for half_of in (0, 1):
                    zz = 2 * jj + half_of
                    hit = relr[yy, pl.ds(zz, 1), :] == spot_row
                    piece = term[half_of * cap : (half_of + 1) * cap, :]
                    ret[yy, pl.ds(zz, 1), :] = jnp.sum(jnp.where(hit, piece, 0.0), axis=0, keepdims=True)
                return carry

            lax.fori_loop(0, ny * nz // 2, finish, 0)
            for j in range(1, ny):
                ret_copy(j).start()
            retr[y] = ret[y]

        @pl.when(tau == chunks + far + 2)
        def _():
            for j in range(1, ny):
                ret_copy(j).wait()
            bz[...] = jnp.zeros_like(bz)
            for zz in range(nz):
                for yy in range(ny):
                    bz[zz, yy : yy + 1, :] = retr[yy, zz : zz + 1, :]
            for j in range(1, nz):
                back_copy(j).start()

        @pl.when(tau == chunks + far + 3)
        def _():
            for j in range(1, nz):
                back_copy(j).wait()
            bk[z] = bz[z]
            back[...] = bk[...]

        return carry

    lax.fori_loop(0, chunks + far + 6, step, 0)


def whole(nx, ny, nz, chunks, meta, share, tok, hid, mas, fst, snd, cap):
    toks, feats = tok.shape
    dk = feats // chunks
    shard = mas.shape[0]
    units = hid.shape[1]
    count = hid.shape[0]
    block = nz * cap
    part = shard // nz
    vmem = pl.BlockSpec(memory_space=pltpu.VMEM)
    dma = pltpu.SemaphoreType.DMA
    n_dma = lambda *s: dma(tuple(max(1, v) for v in s))
    scratch = [
        pltpu.VMEM((chunks, nz, toks, dk), BF),
        pltpu.VMEM((chunks, CORES, nx, shard, dk), BF),
        pltpu.VMEM((2, ny, block, dk), BF),
        pltpu.VMEM((chunks, ny, block, dk), BF),
        pltpu.VMEM((nz // 2, ny * 2 * cap, 2 * toks), BF),
        pltpu.VMEM((count, 128), F32),
        pltpu.VMEM((units, count), BF),
        pltpu.VMEM((count, units), F32),
        pltpu.VMEM((2, nx, shard, dk), BF),
        pltpu.VMEM((chunks, nx, shard, dk), BF),
        pltpu.VMEM((nx, shard, dk), F32),
        pltpu.VMEM((2, nx, shard, dk), BF),
        pltpu.VMEM((chunks, nx, shard, dk), BF),
        pltpu.VMEM((shard, dk), F32),
        pltpu.VMEM((chunks, shard, dk), F32),
        pltpu.VMEM((chunks, nz, part, dk), BF),
        pltpu.VMEM((chunks, nz, part, dk), BF),
        pltpu.VMEM((chunks, HOT, part, dk), BF),
        pltpu.VMEM((chunks, ny, HOT, part, dk), BF),
        pltpu.VMEM((chunks, nz, part, dk), BF),
        pltpu.VMEM((chunks, nz, part, dk), BF),
        pltpu.VMEM((nz, 8, 128), F32),
        pltpu.VMEM((ny, 2 * nz, 128), F32),
        pltpu.VMEM((ny, 2 * nz, 128), F32),
        pltpu.VMEM((ny, nz, 128), F32),
        pltpu.VMEM((ny, nz, 128), F32),
        pltpu.VMEM((nz, 8, 128), F32),
        pltpu.VMEM((nz, 8, 128), F32),
        n_dma(chunks),
        n_dma(2, nz // 2, chunks),
        n_dma(2, nz // 2, chunks),
        n_dma(ny - 1, chunks),
        n_dma(ny - 1, chunks),
        n_dma(nx - 1, chunks),
        n_dma(nx - 1, chunks),
        n_dma(chunks),
        n_dma(chunks),
        n_dma(chunks),
        n_dma(chunks),
        n_dma(nx - 1, chunks),
        n_dma(nx - 1, chunks),
        n_dma(nz - 1, chunks),
        n_dma(nz - 1, chunks),
        n_dma(ny - 1, chunks),
        n_dma(ny - 1, chunks),
        n_dma(nz - 1, chunks),
        n_dma(nz - 1, chunks),
        n_dma(nz - 1),
        n_dma(nz - 1),
        n_dma(ny - 1),
        n_dma(ny - 1),
        n_dma(ny - 1),
        n_dma(ny - 1),
        n_dma(nz - 1),
        n_dma(nz - 1),
    ]
    return pl.pallas_call(
        functools.partial(kernel, nx, ny, nz, chunks, cap),
        out_shape=(
            jax.ShapeDtypeStruct((count, units), BF),
            jax.ShapeDtypeStruct((nz, 8, 128), F32),
            jax.ShapeDtypeStruct((shard, feats), F32),
            jax.ShapeDtypeStruct((shard, feats), BF),
            jax.ShapeDtypeStruct((shard, feats), BF),
        ),
        in_specs=[
            vmem,
            pl.BlockSpec(memory_space=pltpu.SMEM),
            pl.BlockSpec(memory_space=pl.ANY),
            vmem,
            vmem,
            vmem,
            vmem,
        ],
        out_specs=(vmem,) * 5,
        scratch_shapes=scratch,
        compiler_params=pltpu.CompilerParams(
            collective_id=0, has_side_effects=True, vmem_limit_bytes=62 * 2**20
        ),
        cost_estimate=pl.CostEstimate(
            flops=4 * count * units * feats, bytes_accessed=20 * 2**20, transcendentals=0
        ),
    )(meta, share, tok, hid, mas, fst, snd)


def on_device(
    nx,
    ny,
    nz,
    chunks,
    grad_out,
    gate_probs,
    expert_route,
    replica_pick,
    slot_expert,
    saved_hidden,
    master,
    first_moment,
    second_moment,
):
    slots = slot_expert.shape[0]
    cap = saved_hidden.shape[4]
    units = saved_hidden.shape[5]
    toks, top = gate_probs.shape
    ids = jnp.arange(slots, dtype=jnp.int32)
    same = slot_expert[:, None] == slot_expert[None, :]
    rank = jnp.sum(same & (ids[None, :] < ids[:, None]), axis=1)
    host = slot_expert[None, :, None] == expert_route.T[:, None, :]
    copies = jnp.sum(host.astype(jnp.int32), axis=1)
    chosen = host & (rank[None, :, None] == (replica_pick.T % copies)[:, None, :])
    taken = jnp.any(chosen, axis=0)
    order = jnp.arange(toks, dtype=jnp.int32)
    before = (order[:, None] < order[None, :]).astype(BF)
    place = jnp.dot(taken.astype(BF), before, preferred_element_type=F32)
    spot = jnp.where(taken, place, -1.0)
    gates = gate_probs.T.astype(BF).astype(F32)
    gate_of = jnp.sum(jnp.where(chosen, gates[:, None, :], 0.0), axis=0)
    meta = jnp.concatenate([spot.reshape(nz, ny, toks), gate_of.reshape(nz, ny, toks)], axis=1)
    if 2 * ny < 8:
        meta = jnp.pad(meta, ((0, 0), (0, 8 - 2 * ny), (0, 0)))
    share = (slot_expert[None, :] == jnp.arange(HOT, dtype=jnp.int32)[:, None]).astype(F32)
    hidden = saved_hidden.reshape(nz, ny, cap, units).transpose(1, 0, 2, 3).reshape(slots * cap, units)
    hidden_grad, back, new_master, new_first, new_second = whole(
        nx, ny, nz, chunks, meta, share, grad_out, hidden, master[0], first_moment[0], second_moment[0], cap
    )
    by_slot = back[:, :ny, :].reshape(slots, toks)
    gate_grad = jnp.sum(jnp.where(chosen, by_slot[None], 0.0), axis=1).T
    hidden_grad = hidden_grad.reshape(ny, nz, cap, units).transpose(1, 0, 2, 3).reshape(saved_hidden.shape)
    return hidden_grad, gate_grad, new_master[None], new_first[None], new_second[None]


def build(mesh, nx, ny, nz, chunks):
    tokens = P(("dp", "expert"), None)
    acts = P("dp", "expert", None, None, None, None)
    shard = P("expert", "dp", None)
    return jax.shard_map(
        functools.partial(on_device, nx, ny, nz, chunks),
        mesh=mesh,
        in_specs=(tokens, tokens, tokens, tokens, P(), acts, shard, shard, shard),
        out_specs=(acts, tokens, shard, shard, shard),
        check_vma=False,
    )


def solution(mesh):
    ny = 4
    return build(mesh, mesh.shape["dp"] // CORES, ny, mesh.shape["expert"] // ny, 7)
```

time: 334 us -> 176 us (0.53)
  waiting for transfers between devices: 194 us -> 0 us
  Pallas kernels: 0 us -> 157 us
  blocking collectives: 49 us -> 0 us
  starting transfers between devices: 29.5 us -> 0 us
  matrix products: 26.1 us -> 0.13 us
  between operations: 14.2 us -> 0.7 us
  other arithmetic: 14 us -> 7.25 us
    pallas_call x0 -> x1, Pallas kernels: none -> 157 us  [whole(): pl.pallas_call(functools.partial(kernel, nx, ny, nz, chunks, cap), out_sh...]
    all_to_all x3 -> x0, waiting for transfers between devices: 152 us -> none  [the longest x1 121 us: on_device(): lax.all_to_all(send_rows.reshape(slots, cap, feats), 'expert', split_axis...]
    all_to_all x2 -> x0, blocking collectives: 49 us -> none  [the longest x1 36.3 us: on_device(): lax.all_to_all(reduced.reshape(slots, part, feats), 'expert', split_axis=...]
    reduce_scatter x1 -> x0, waiting for transfers between devices: 42.2 us -> none  [on_device(): reduced = lax.psum_scatter(partial, 'dp', scatter_dimension=0, tiled=True)]
    all_to_all x3 -> x0, starting transfers between devices: 29.4 us -> none  [the longest x1 11.7 us: on_device(): lax.all_to_all(send_rows.reshape(slots, cap, feats), 'expert', split_axis...]
    dot_general x5 -> x1, matrix products: 26.1 us -> 0.13 us  [on_device(): place = jnp.dot(taken.astype(BF), before, preferred_element_type=F32)]
    convert_element_type x7 -> x2, other arithmetic: 12.3 us -> 1.93 us  [the longest x1 1.24 us: on_device(): (slot_expert[None, :] == jnp.arange(HOT, dtype=jnp.int32)[:, None]).astyp...]
    convert_element_type x4 -> x0, local copies, waits for them, and re-layouts: 4.39 us -> none  [the longest x1 2.57 us: on_device(): total = back.reshape(1, rows_own, feats).astype(jnp.float32)]
  transfers between devices with their start and end apart: 5 -> 0, of which waited for: 4 -> 0; matrix products, arithmetic and copies ran while one was open for 3% -> 0% of each run, Pallas kernels for 0% -> 0%
where the time goes in v2:
time: 176 us; the launch traced here: 174 us
  Pallas kernels  157 us (89%)
  local copies, waits for them, and re-layouts  9.83 us (6%)
  other arithmetic  7.25 us (4%)
    pallas_call x1, Pallas kernels, whole(): pl.pallas_call(functools.partial(kernel, nx, ny, nz, chunks, cap), out_sh...  157 us
    unnamed x15, local copies, waits for them, and re-layouts  4.27 us

profile of v2, /device:TPU:2, one launch (start us, length us, event | category | flops | bytes accessed | tf_op | source)
XLA Modules:
  0.0 174.4 jit_solution(16174394120589249803)
XLA Ops:
  0.6 0.9 convert_reduce_fusion
  1.5 0.7 convert_bitcast_fusion
  2.2 0.8 fusion
  3.0 0.8 add_select_fusion
  3.8 1.2 fusion.3.share
  5.0 0.8 fusion.1
  5.8 0.1 convolution_select_fusion
  6.0 0.8 select_reduce_fusion.1
  6.7 0.6 pad_maximum_fusion.meta
  7.4 2.7 %copy.16 = bf16[8,4,24,1024]{3,2,0,1:T(8,128)(2,1)} copy(bf16[8,4,24,1024]{3,2,1,0:T(8,128)(2,1)} %bitcast.27) | data formatting | bytes 3145728 | tf_op jit(solution)/shard_map/reshape | solution.py:599
  10.1 156.5 %shard_map.128 = (bf16[768,1024]{1,0:T(8,128)(2,1)}, f32[8,8,128]{2,1,0:T(8,128)}, f32[128,3584]{1,0:T(8,128)}, bf16[128,3584]{1,0:T(8,128)(2,1)}, bf16[128,3584]{1,0:T(8,128)(2,1)}) custom-call(f32[8,8,128]{2,1,0:T(8,128)} %pad_maximum_fusion.meta, f32[3,32]{1,0:T(4,128)} %fusion.3.share, bf16[128,3584]{1,0:T(8,128)(2,1)} %tok.1, ...), custom_call_target="tpu_custom_call" | custom-call | flops 11274289152 | bytes 20971520 | tf_op jit(solution)/shard_map/pallas_call | solution.py:534
  166.6 0.0 copy-start.5
  166.6 0.0 copy-start.3
  166.6 0.0 copy-start.4
  166.6 0.0 copy-start
  166.6 2.8 %copy.17 = bf16[8,4,24,1024]{3,2,1,0:T(8,128)(2,1)} copy(bf16[8,4,24,1024]{3,2,0,1:T(8,128)(2,1)} %bitcast.29) | data formatting | bytes 3145728 | tf_op jit(solution)/shard_map/transpose | solution.py:605
  169.5 0.0 copy-done.5
  169.5 0.0 copy-done.3
  169.5 0.0 copy-done.4
  169.5 0.7 select_reduce_fusion
  170.2 0.0 copy-done
  170.2 0.0 copy-start.2
  170.2 1.2 copy.21
  171.4 0.6 copy-done.2
  172.0 0.0 copy-start.1
  172.0 0.9 copy.22
  172.9 0.6 copy-done.1
  173.5 0.9 copy.23
  (1 shorter events, 0.0 us)
Async XLA Ops:
  166.6 2.9 %copy-start.5 = (f32[8,8,128]{2,1,0:T(8,128)S(1)}, f32[8,8,128]{2,1,0:T(8,128)}, u32[]{:S(2)}) copy-start(f32[8,8,128]{2,1,0:T(8,128)} %get-tuple-element.11) | copy-start | bytes 98308
  166.6 2.9 %copy-start.3 = (s32[128,4]{0,1:T(4,128)S(1)}, s32[128,4]{0,1:T(4,128)}, u32[]{:S(2)}) copy-start(s32[128,4]{0,1:T(4,128)} %param.11) | copy-start | bytes 6148
  166.6 2.9 %copy-start.4 = (s32[32]{0:T(128)S(1)}, s32[32]{0:T(128)}, u32[]{:S(2)}) copy-start(s32[32]{0:T(128)} %param.13) | copy-start | bytes 388
  166.6 3.6 %copy-start = (f32[128,3584]{1,0:T(8,128)S(1)}, f32[128,3584]{1,0:T(8,128)}, u32[]{:S(2)}) copy-start(f32[128,3584]{1,0:T(8,128)} %get-tuple-element.12) | copy-start | bytes 5505028
  170.2 1.8 %copy-start.2 = (bf16[128,3584]{1,0:T(8,128)(2,1)S(1)}, bf16[128,3584]{1,0:T(8,128)(2,1)}, u32[]{:S(2)}) copy-start(bf16[128,3584]{1,0:T(8,128)(2,1)} %get-tuple-element.13) | copy-start | bytes 2752516
  172.0 1.5 copy-start.1

commit v3 on v2

v3 whole, which is shorter than its diff:
```python
import functools

import jax
import jax.numpy as jnp
from jax import lax
from jax.experimental import pallas as pl
from jax.experimental.pallas import tpu as pltpu
from jax.sharding import PartitionSpec as P

HOT = 3
CORES = 2
AHEAD = 1
SLACK = 2
BF = jnp.bfloat16
F32 = jnp.float32
MESH = pl.DeviceIdType.MESH

beta_one = 0.9
beta_two = 0.95
learn_rate = 0.00022
decay_rate = 0.1
epsilon = 1e-08
correct_one = 0.6513215599
correct_two = 0.4012630607


def kernel(
    nx,
    ny,
    nz,
    chunks,
    cap,
    holder,
    route,
    pick,
    prob,
    tok,
    hid_in,
    mas_in,
    fst_in,
    snd_in,
    hg_out,
    gg,
    nm_out,
    nf_out,
    ns_out,
    hid,
    mas,
    fst,
    snd,
    hg,
    nm,
    nf,
    ns,
    chosen,
    taken,
    meta,
    xg,
    wg,
    sendy,
    rows,
    pick2,
    gcol,
    gated,
    proj,
    csend,
    crecv,
    ownh,
    xsend,
    xrecv,
    xown,
    gsh,
    hs1,
    hr1,
    ts,
    tr,
    hs2,
    hr2,
    mz,
    rel,
    relr,
    ret,
    retr,
    bz,
    bk,
    load_sem,
    mas_sem,
    in_sem,
    hid_sem,
    out_sem,
    hg_sem,
    zs,
    zr,
    ys,
    yr,
    wxs,
    wxr,
    wcs,
    wcr,
    cs,
    cr,
    xs,
    xr,
    h1s,
    h1r,
    tss,
    tsr,
    h2s,
    h2r,
    ms,
    mr,
    rs,
    rr,
    qs,
    qr,
    bs,
    br,
):
    p, q = lax.axis_index("dp"), lax.axis_index("expert")
    x, c = p // CORES, lax.rem(p, CORES)
    z, y = q // ny, lax.rem(q, ny)
    toks = xg.shape[2]
    dk = xg.shape[3]
    shard = wg.shape[3]
    far, near = nz // 2, nz - 1 - nz // 2
    block = nz * cap
    pair = 2 * cap
    part = shard // nz
    picked = far + AHEAD

    at_x = [lax.rem(x + j, nx) for j in range(nx)]
    at_y = [lax.rem(y + j, ny) for j in range(ny)]
    at_z = [lax.rem(z + j, nz) for j in range(nz)]
    to_x = [v * CORES + c for v in at_x]
    to_y = [z * ny + v for v in at_y]
    to_z = [v * ny + y for v in at_z]
    other = x * CORES + 1 - c

    def remote(src, dst, ssem, rsem, pp, qq):
        return pltpu.make_async_remote_copy(
            src_ref=src, dst_ref=dst, send_sem=ssem, recv_sem=rsem, device_id=(pp, qq), device_id_type=MESH
        )

    def lanes(k):
        return pl.ds(pl.multiple_of(k * dk, 128), dk)

    def load(k):
        return pltpu.make_async_copy(tok.at[:, lanes(k)], xg.at[k, z], load_sem.at[k])

    def load_hid(yy):
        return pltpu.make_async_copy(hid_in.at[:, yy], hid.at[yy], hid_sem.at[yy])

    def save_hg(yy):
        return pltpu.make_async_copy(hg.at[yy], hg_out.at[:, yy], hg_sem.at[yy])

    load_mas = pltpu.make_async_copy(mas_in, mas, mas_sem.at[0])
    loads = [
        pltpu.make_async_copy(fst_in, fst, in_sem.at[0]),
        pltpu.make_async_copy(snd_in, snd, in_sem.at[1]),
    ]

    def saves(k):
        return [
            pltpu.make_async_copy(src.at[:, lanes(k)], dst.at[:, lanes(k)], out_sem.at[i, k])
            for i, (src, dst) in enumerate(((nm, nm_out), (nf, nf_out), (ns, ns_out)))
        ]

    load(0).start()
    def share(e, s):
        return jnp.where(holder[s] == e, 1.0, 0.0)

    barrier = pltpu.get_barrier_semaphore()
    peers = [(p, v) for v in to_z[1:] + to_y[1:]] + [(v, q) for v in to_x[1:]] + [(other, q)]
    for peer in peers:
        pl.semaphore_signal(barrier, inc=1, device_id=peer, device_id_type=MESH)
    for k in range(1, chunks):
        load(k).start()
    load_mas.start()
    for yy in range(ny):
        load_hid(yy).start()
    for copy in loads:
        copy.start()
    pl.semaphore_wait(barrier, len(peers))

    def meta_copy(j):
        return remote(meta.at[at_z[j]], mz.at[z], ms.at[0], mr.at[0], p, to_z[j])

    def meta_all():
        return remote(meta.at[pl.ds(0, nz - 1)], mz.at[pl.ds(0, nz - 1)], ms.at[0], mr.at[0], p, to_z[1])

    def rel_copy(j):
        return remote(rel.at[at_y[j]], relr.at[y], rs.at[0], rr.at[0], p, to_y[j])

    def rel_all():
        return remote(rel.at[pl.ds(0, ny - 1)], relr.at[pl.ds(0, ny - 1)], rs.at[0], rr.at[0], p, to_y[1])

    def ret_copy(j):
        return remote(ret.at[at_y[j]], retr.at[y], qs.at[0], qr.at[0], p, to_y[j])

    def ret_all():
        return remote(ret.at[pl.ds(0, ny - 1)], retr.at[pl.ds(0, ny - 1)], qs.at[0], qr.at[0], p, to_y[1])

    def back_copy(j):
        return remote(bz.at[at_z[j]], bk.at[z], bs.at[0], br.at[0], p, to_z[j])

    def back_all():
        return remote(bz.at[pl.ds(0, nz - 1)], bk.at[pl.ds(0, nz - 1)], bs.at[0], br.at[0], p, to_z[1])

    origins = ([at_z[-h % nz] for h in range(far)], [at_z[h % nz] for h in range(far)])
    nexts = (to_z[1], to_z[nz - 1])

    def hop(d, h, k):
        if isinstance(d, int):
            origin, to = origins[d][h - 1], nexts[d]
        else:
            origin = jnp.where(d == 0, origins[0][h - 1], origins[1][h - 1])
            to = jnp.where(d == 0, nexts[0], nexts[1])
        return remote(xg.at[k, origin], xg.at[k, origin], zs.at[d, h - 1, k], zr.at[d, h - 1, k], p, to)

    def forward(h, k, wait):
        for d in (0, 1):
            if h <= near:
                if wait:
                    hop(d, h, k).wait()
                if h + 1 <= near:
                    hop(d, h + 1, k).start()
        if h == near and near < far:
            hop(lax.rem(k, 2), far, k).start()
        if h > near and wait:
            hop(lax.rem(k, 2), far, k).wait()

    cut = max(1, chunks // 2)
    pieces = [(0, cut), (cut, chunks - cut)]

    def weight_copy(j, i):
        here = pl.ds(*pieces[i])
        return remote(wg.at[here, c, x], wg.at[here, c, x], wxs.at[i], wxr.at[i], to_x[j], q)

    def weight_all(i):
        here, most = pl.ds(*pieces[i]), pl.ds(0, nx - 1)
        return remote(wg.at[here, c, most], wg.at[here, c, most], wxs.at[i], wxr.at[i], to_x[1], q)

    def weight_pass(i):
        here = pl.ds(*pieces[i])
        return remote(wg.at[here, c], wg.at[here, c], wcs.at[i], wcr.at[i], other, q)

    def row_copy(j, k, slot):
        return remote(sendy.at[slot, at_y[j]], rows.at[k, y], ys.at[k], yr.at[k], p, to_y[j])

    def row_all(k):
        most = pl.ds(0, ny - 1)
        return remote(sendy.at[0, most], rows.at[k, most], ys.at[k], yr.at[k], p, to_y[1])

    def core_copy(k):
        return remote(csend.at[lax.rem(k, SLACK)], crecv.at[k], cs.at[k], cr.at[k], other, q)

    def x_copy(j, k):
        return remote(
            xsend.at[lax.rem(k, SLACK), at_x[j]], xrecv.at[k, x], xs.at[k], xr.at[k], to_x[j], q
        )

    def x_all(k):
        most = pl.ds(0, nx - 1)
        return remote(xsend.at[0, most], xrecv.at[k, most], xs.at[k], xr.at[k], to_x[1], q)

    def first_copy(j, k, n):
        here = pl.ds(k, n)
        return remote(hs1.at[here, at_z[j]], hr1.at[here, z], h1s.at[k], h1r.at[k], p, to_z[j])

    def first_all(k, n):
        here, most = pl.ds(k, n), pl.ds(0, nz - 1)
        return remote(hs1.at[here, most], hr1.at[here, most], h1s.at[k], h1r.at[k], p, to_z[1])

    def table_copy(j, k, n):
        here = pl.ds(k, n)
        return remote(ts.at[here], tr.at[here, y], tss.at[k], tsr.at[k], p, to_y[j])

    def table_all(k, n):
        here, most = pl.ds(k, n), pl.ds(0, ny - 1)
        return remote(tr.at[here, most], tr.at[here, most], tss.at[k], tsr.at[k], p, to_y[1])

    def second_copy(j, k, n):
        here = pl.ds(k, n)
        return remote(hs2.at[here, at_z[j]], hr2.at[here, z], h2s.at[k], h2r.at[k], p, to_z[j])

    def second_all(k, n):
        here, most = pl.ds(k, n), pl.ds(0, nz - 1)
        return remote(hs2.at[here, most], hr2.at[here, most], h2s.at[k], h2r.at[k], p, to_z[1])

    def when(k):
        return pl.when((k >= 0) & (k < chunks))

    def grouped(k):
        def run(body):
            pl.when((k >= 0) & (k < chunks) & (lax.rem(k, 2) == 1))(lambda: body(k - 1, 2))
            if chunks % 2:
                pl.when(k == chunks - 1)(lambda: body(chunks - 1, 1))

        return run

    spot_row = lax.broadcasted_iota(jnp.int32, (cap, toks), 0).astype(F32)

    def step_of(k):
        flag = share(0, q)
        for e in range(1, HOT):
            flag = flag + share(e, q)

        @pl.when(k == 0)
        def _():
            for copy in loads:
                copy.wait()

        def adam(b, carry):
            here = pl.ds(pl.multiple_of(b * part, part), part)
            grad = flag * hr2[k, b].astype(F32) + (1.0 - flag) * gsh[k, here, :]
            old = mas[here, lanes(k)]
            first = beta_one * fst[here, lanes(k)].astype(F32) + (1.0 - beta_one) * grad
            second = beta_two * snd[here, lanes(k)].astype(F32) + (1.0 - beta_two) * grad * grad
            update = first / correct_one / (jnp.sqrt(second / correct_two) + epsilon) + decay_rate * old
            nm[here, lanes(k)] = old - learn_rate * update
            nf[here, lanes(k)] = first.astype(BF)
            ns[here, lanes(k)] = second.astype(BF)
            return carry

        lax.fori_loop(0, nz, adam, 0)
        for copy in saves(k):
            copy.start()


    def step(tau, carry):
        for h in range(far, 0, -1):

            @when(tau - AHEAD - h)
            def _(h=h, k=tau - AHEAD - h):
                forward(h, k, True)

        @when(tau)
        def _(k=tau):
            load(k).wait()
            for d in (0, 1):
                if near:
                    hop(d, 1, k).start()
            if not near:
                hop(lax.rem(k, 2), 1, k).start()

        @pl.when(tau == AHEAD)
        def _():
            load_mas.wait()
            for k in range(chunks):
                wg[k, c, x] = mas[:, k * dk : (k + 1) * dk].astype(BF)
            for i in (0, 1):
                for j in range(1, nx):
                    weight_copy(j, i).start()

        for i, at in ((0, picked + SLACK - 2), (1, picked + SLACK - 1 + cut // 2)):

            @pl.when(tau == at)
            def _(i=i):
                if nx > 1:
                    weight_all(i).wait()
                weight_pass(i).start()

        @pl.when(tau == AHEAD)
        def _():
            slots = nz * ny
            named = route[...]

            def count(s, carry):
                return carry + jnp.where(named == holder[s], 1.0, 0.0)

            copies = lax.fori_loop(0, slots, count, jnp.zeros(named.shape, F32))
            wanted = pick[...].astype(F32)
            wanted = wanted - copies * jnp.floor((wanted + 0.5) / copies)
            gates = prob[...].astype(BF).astype(F32)
            meta[...] = jnp.zeros_like(meta)

            def assign(s, seen):
                host = jnp.where(named == holder[s], 1.0, 0.0)
                hit = host * jnp.where(seen == wanted, 1.0, 0.0)
                chosen[s] = hit
                taken[pl.ds(s, 1), :] = jnp.sum(hit, axis=0, keepdims=True)
                meta[s // ny, pl.ds(ny + lax.rem(s, ny), 1), :] = jnp.sum(hit * gates, axis=0, keepdims=True)
                return seen + host

            lax.fori_loop(0, slots, assign, jnp.zeros(named.shape, F32))
            before = jnp.where(
                lax.broadcasted_iota(jnp.int32, (toks, toks), 0)
                < lax.broadcasted_iota(jnp.int32, (toks, toks), 1),
                1.0,
                0.0,
            ).astype(BF)
            place = jnp.dot(taken[...].astype(BF), before, preferred_element_type=F32)
            spot = jnp.where(taken[...] > 0.5, place, -1.0)
            for s in range(slots):
                meta[s // ny, s % ny : s % ny + 1, :] = spot[s : s + 1, :]
            for j in range(1, nz):
                meta_copy(j).start()
            mz[z] = meta[z]

        @pl.when(tau == AHEAD + 1)
        def _():
            meta_all().wait()
            for yy in range(ny):
                for zz in range(nz):
                    rel[yy, zz : zz + 1, :] = mz[zz, yy : yy + 1, :]
                    rel[yy, nz + zz : nz + zz + 1, :] = mz[zz, ny + yy : ny + yy + 1, :]
            for j in range(1, ny):
                rel_copy(j).start()
            relr[y] = rel[y]
            zero = jnp.zeros((cap, toks), F32)
            for jj in range(nz // 2):
                for yy in range(ny):
                    one = [
                        jnp.where(mz[2 * jj + i, yy : yy + 1, :] == spot_row, 1.0, 0.0) for i in (0, 1)
                    ]
                    top = jnp.concatenate([one[0], zero], axis=1)
                    low = jnp.concatenate([zero, one[1]], axis=1)
                    pick2[jj, yy * pair : (yy + 1) * pair, :] = jnp.concatenate([top, low], axis=0).astype(BF)

        begin, room = AHEAD + 2, picked + SLACK - AHEAD - 2

        @pl.when(tau == begin)
        def _():
            rel_all().wait()
            for yy in range(ny):
                load_hid(yy).wait()

        for yy in range(ny):

            @pl.when(tau == begin + yy * (room - 1) // ny)
            def _(yy=yy):
                def scale(zz, carry):
                    here = pl.ds(pl.multiple_of(yy * block + zz * cap, 8), cap)
                    hit = relr[yy, pl.ds(zz, 1), :] == spot_row
                    gate = jnp.where(hit, relr[yy, pl.ds(nz + zz, 1), :], 0.0)
                    column = jnp.sum(gate, axis=1, keepdims=True)
                    gcol[here, :] = jnp.broadcast_to(column, (cap, 128))
                    proj[here, :] = hid[yy, zz].astype(F32) * column
                    return carry

                lax.fori_loop(0, nz, scale, 0)

        @pl.when(tau == begin + room - 1)
        def _():
            def turn(i, carry):
                here = pl.ds(pl.multiple_of(i * 128, 128), 128)
                turned = proj[here, :].T.astype(BF)
                for core in range(CORES):
                    for xx in range(nx):
                        start = (xx * CORES + core) * shard
                        gated[core, xx * shard : (xx + 1) * shard, here] = turned[start : start + shard, :]
                return carry

            lax.fori_loop(0, ny * block // 128, turn, 0)
            proj[...] = jnp.zeros_like(proj)

        @when(tau - picked)
        def _(k=tau - picked):
            slot = lax.rem(k, SLACK + 1)

            def choose(jj, carry):
                two = xg[k, pl.ds(2 * jj, 2)].reshape(2 * toks, dk)
                got = jnp.dot(pick2[jj], two, preferred_element_type=F32).astype(BF)
                here = pl.ds(pl.multiple_of(jj * pair, pair), pair)
                for yy in range(ny):
                    sendy[slot, yy, here, :] = got[yy * pair : (yy + 1) * pair, :]
                return carry

            lax.fori_loop(0, nz // 2, choose, 0)
            for j in range(1, ny):
                row_copy(j, k, slot).start()
            rows[k, y] = sendy[slot, y]

        @grouped(tau - picked - 5 * SLACK)
        def _(k0, n):
            table_all(k0, n).wait()
            for i in range(n):
                k = k0 + i
                total = []
                for e in range(HOT):
                    acc = tr[k, 0, e].astype(F32)
                    for yy in range(1, ny):
                        acc = acc + tr[k, yy, e].astype(F32)
                    total.append(acc)
                for zz in range(nz):
                    acc = share(0, zz * ny + y) * total[0]
                    for e in range(1, HOT):
                        acc = acc + share(e, zz * ny + y) * total[e]
                    hs2[k, zz] = acc.astype(BF)
            for j in range(1, nz):
                second_copy(j, k0, n).start()
            for i in range(n):
                hr2[k0 + i, z] = hs2[k0 + i, z]

        @grouped(tau - picked - 4 * SLACK)
        def _(k0, n):
            first_all(k0, n).wait()
            for i in range(n):
                k = k0 + i
                sums = [jnp.zeros((part, dk), F32)] * HOT
                for zz in range(nz):
                    value = hr1[k, zz].astype(F32)
                    sums = [sums[e] + share(e, zz * ny + y) * value for e in range(HOT)]
                for e in range(HOT):
                    ts[k, e] = sums[e].astype(BF)
            for j in range(1, ny):
                table_copy(j, k0, n).start()
            for i in range(n):
                tr[k0 + i, y] = ts[k0 + i]

        @when(tau - picked - 3 * SLACK)
        def _(k=tau - picked - 3 * SLACK):
            if nx > 1:
                x_all(k).wait()

            def add(b, carry):
                here = pl.ds(pl.multiple_of(b * part, part), part)
                value = xown[lax.rem(k, SLACK), here, :]
                for j in range(1, nx):
                    value = value + xrecv[k, at_x[nx - j], here, :].astype(F32)
                gsh[k, here, :] = value
                hs1[k, b] = value.astype(BF)
                return carry

            lax.fori_loop(0, nz, add, 0)
            hr1[k, z] = hs1[k, z]

        @grouped(tau - picked - 3 * SLACK)
        def _(k0, n):
            for j in range(1, nz):
                first_copy(j, k0, n).start()

        @when(tau - picked - 2 * SLACK)
        def _(k=tau - picked - 2 * SLACK):
            slot = lax.rem(k, SLACK)
            core_copy(k).wait()
            for j in range(1, nx):
                xsend[slot, at_x[j]] = (
                    ownh[slot, at_x[j]].astype(F32) + crecv[k, at_x[j]].astype(F32)
                ).astype(BF)
                x_copy(j, k).start()
            xown[slot] = ownh[slot, x].astype(F32) + crecv[k, x].astype(F32)

        @when(tau - picked - 1 * SLACK)
        def _(k=tau - picked - 1 * SLACK):
            row_all(k).wait()
            slot = lax.rem(k, SLACK)

            tile = min(256, dk)

            def half(core, out):
                def columns(t, carry):
                    here = pl.ds(pl.multiple_of(t * tile, tile), tile)
                    got = jnp.dot(
                        gated[core],
                        rows[k, :, :, here].reshape(ny * block, tile),
                        preferred_element_type=F32,
                    )
                    out[slot, :, :, here] = got.astype(BF).reshape(nx, shard, tile)
                    return carry

                lax.fori_loop(0, dk // tile, columns, 0)

            def project(xx, carry):
                w = jnp.concatenate([wg[k, 0, xx], wg[k, 1, xx]], axis=0)
                here = pl.ds(pl.multiple_of(xx * CORES * shard, CORES * shard), CORES * shard)
                proj[:, here] += lax.dot_general(
                    rows[k].reshape(ny * block, dk), w, (((1,), (1,)), ((), ())), preferred_element_type=F32
                )
                return carry

            half(1 - c, csend)
            core_copy(k).start()
            half(c, ownh)
            for i in (0, 1):

                @pl.when(k == pieces[i][0])
                def _(i=i):
                    weight_pass(i).wait()

            lax.fori_loop(0, nx, project, 0)

        @grouped(tau - picked - 6 * SLACK)
        def _(k0, n):
            second_all(k0, n).wait()
            for i in range(n):
                step_of(k0 + i)

        last = chunks + picked + SLACK

        for yy in range(ny):

            @pl.when(tau == last + yy)
            def _(yy=yy):
                def finish(zz, carry):
                    here = pl.ds(pl.multiple_of(yy * block + zz * cap, 8), cap)
                    value = proj[here, :]
                    hg[yy, zz] = (gcol[here, :][:, 0:1] * value).astype(BF)
                    term = jnp.sum(hid[yy, zz].astype(F32) * value, axis=1, keepdims=True)
                    hit = relr[yy, pl.ds(zz, 1), :] == spot_row
                    ret[yy, pl.ds(zz, 1), :] = jnp.sum(jnp.where(hit, term, 0.0), axis=0, keepdims=True)
                    return carry

                lax.fori_loop(0, nz, finish, 0)
                save_hg(yy).start()

        @pl.when(tau == last + ny - 1)
        def _():
            for j in range(1, ny):
                ret_copy(j).start()
            retr[y] = ret[y]

        @pl.when(tau == last + ny)
        def _():
            ret_all().wait()
            bz[...] = jnp.zeros_like(bz)
            for zz in range(nz):
                for yy in range(ny):
                    bz[zz, yy : yy + 1, :] = retr[yy, zz : zz + 1, :]
            for j in range(1, nz):
                back_copy(j).start()
            bk[z] = bz[z]

        @pl.when(tau == last + ny + 1)
        def _():
            back_all().wait()
            total = jnp.zeros(gg.shape, F32)
            for s in range(nz * ny):
                total = total + chosen[s] * bk[s // ny, s % ny : s % ny + 1, :]
            gg[...] = total

        return carry

    lax.fori_loop(0, chunks + picked + max(6 * SLACK, SLACK + ny + 2), step, 0)
    for k in range(chunks):
        for copy in saves(k):
            copy.wait()
    for yy in range(ny):
        save_hg(yy).wait()


def whole(nx, ny, nz, chunks, holder, route, pick, prob, tok, hid, mas, fst, snd):
    toks, feats = tok.shape
    dk = feats // chunks
    shard = mas.shape[0]
    cap, units = hid.shape[2:]
    slots = nz * ny
    count = slots * cap
    block = nz * cap
    part = shard // nz
    top = route.shape[0]
    hbm = pl.BlockSpec(memory_space=pl.ANY)
    vmem = pl.BlockSpec(memory_space=pltpu.VMEM)
    dma = pltpu.SemaphoreType.DMA
    n_dma = lambda *s: dma(tuple(max(1, v) for v in s))
    scratch = [
        pltpu.VMEM((ny, nz, cap, units), BF),
        pltpu.VMEM((shard, feats), F32),
        pltpu.VMEM((shard, feats), BF),
        pltpu.VMEM((shard, feats), BF),
        pltpu.VMEM((ny, nz, cap, units), BF),
        pltpu.VMEM((shard, feats), F32),
        pltpu.VMEM((shard, feats), BF),
        pltpu.VMEM((shard, feats), BF),
        pltpu.VMEM((slots, top, toks), F32),
        pltpu.VMEM((slots, toks), F32),
        pltpu.VMEM((nz, 8, toks), F32),
        pltpu.VMEM((chunks, nz, toks, dk), BF),
        pltpu.VMEM((chunks, CORES, nx, shard, dk), BF),
        pltpu.VMEM((SLACK + 1, ny, block, dk), BF),
        pltpu.VMEM((chunks, ny, block, dk), BF),
        pltpu.VMEM((nz // 2, ny * 2 * cap, 2 * toks), BF),
        pltpu.VMEM((count, 128), F32),
        pltpu.VMEM((CORES, units // CORES, count), BF),
        pltpu.VMEM((count, units), F32),
        pltpu.VMEM((SLACK, nx, shard, dk), BF),
        pltpu.VMEM((chunks, nx, shard, dk), BF),
        pltpu.VMEM((SLACK, nx, shard, dk), BF),
        pltpu.VMEM((SLACK, nx, shard, dk), BF),
        pltpu.VMEM((chunks, nx, shard, dk), BF),
        pltpu.VMEM((SLACK, shard, dk), F32),
        pltpu.VMEM((chunks, shard, dk), F32),
        pltpu.VMEM((chunks, nz, part, dk), BF),
        pltpu.VMEM((chunks, nz, part, dk), BF),
        pltpu.VMEM((chunks, HOT, part, dk), BF),
        pltpu.VMEM((chunks, ny, HOT, part, dk), BF),
        pltpu.VMEM((chunks, nz, part, dk), BF),
        pltpu.VMEM((chunks, nz, part, dk), BF),
        pltpu.VMEM((nz, 8, 128), F32),
        pltpu.VMEM((ny, 2 * nz, 128), F32),
        pltpu.VMEM((ny, 2 * nz, 128), F32),
        pltpu.VMEM((ny, nz, 128), F32),
        pltpu.VMEM((ny, nz, 128), F32),
        pltpu.VMEM((nz, 8, 128), F32),
        pltpu.VMEM((nz, 8, 128), F32),
        n_dma(chunks),
        n_dma(chunks),
        n_dma(2),
        n_dma(ny),
        n_dma(3, chunks),
        n_dma(ny),
        n_dma(2, nz // 2, chunks),
        n_dma(2, nz // 2, chunks),
        n_dma(chunks),
        n_dma(chunks),
        n_dma(chunks),
        n_dma(chunks),
        n_dma(chunks),
        n_dma(chunks),
        n_dma(chunks),
        n_dma(chunks),
        n_dma(chunks),
        n_dma(chunks),
        n_dma(chunks),
        n_dma(chunks),
        n_dma(chunks),
        n_dma(chunks),
        n_dma(chunks),
        n_dma(chunks),
        n_dma(1),
        n_dma(1),
        n_dma(1),
        n_dma(1),
        n_dma(1),
        n_dma(1),
        n_dma(1),
        n_dma(1),
    ]
    return pl.pallas_call(
        functools.partial(kernel, nx, ny, nz, chunks, cap),
        out_shape=(
            jax.ShapeDtypeStruct((nz, ny, cap, units), BF),
            jax.ShapeDtypeStruct((top, toks), F32),
            jax.ShapeDtypeStruct((shard, feats), F32),
            jax.ShapeDtypeStruct((shard, feats), BF),
            jax.ShapeDtypeStruct((shard, feats), BF),
        ),
        in_specs=[pl.BlockSpec(memory_space=pltpu.SMEM), vmem, vmem, vmem, hbm, hbm, hbm, hbm, hbm],
        out_specs=(hbm, vmem, hbm, hbm, hbm),
        scratch_shapes=scratch,
        compiler_params=pltpu.CompilerParams(
            collective_id=0, has_side_effects=True, vmem_limit_bytes=62 * 2**20
        ),
        cost_estimate=pl.CostEstimate(
            flops=4 * count * units * feats, bytes_accessed=20 * 2**20, transcendentals=0
        ),
    )(holder, route, pick, prob, tok, hid, mas, fst, snd)


def on_device(
    nx,
    ny,
    nz,
    chunks,
    grad_out,
    gate_probs,
    expert_route,
    replica_pick,
    slot_expert,
    saved_hidden,
    master,
    first_moment,
    second_moment,
):
    cap, units = saved_hidden.shape[4:]
    hidden_grad, gate_grad, new_master, new_first, new_second = whole(
        nx,
        ny,
        nz,
        chunks,
        slot_expert,
        expert_route.T,
        replica_pick.T,
        gate_probs.T,
        grad_out,
        saved_hidden.reshape(nz, ny, cap, units),
        master[0],
        first_moment[0],
        second_moment[0],
    )
    return (
        hidden_grad.reshape(saved_hidden.shape),
        gate_grad.T,
        new_master[None],
        new_first[None],
        new_second[None],
    )


def build(mesh, nx, ny, nz, chunks):
    tokens = P(("dp", "expert"), None)
    acts = P("dp", "expert", None, None, None, None)
    shard = P("expert", "dp", None)
    return jax.shard_map(
        functools.partial(on_device, nx, ny, nz, chunks),
        mesh=mesh,
        in_specs=(tokens, tokens, tokens, tokens, P(), acts, shard, shard, shard),
        out_specs=(acts, tokens, shard, shard, shard),
        check_vma=False,
    )


def solution(mesh):
    ny = 4
    return build(mesh, mesh.shape["dp"] // CORES, ny, mesh.shape["expert"] // ny, 7)
```

time: 176 us -> 160 us (0.909)
  other arithmetic: 7.25 us -> 0 us
  Pallas kernels: 157 us -> 151 us
  local copies, waits for them, and re-layouts: 9.83 us -> 7.64 us
    pallas_call x1, Pallas kernels: 157 us -> 151 us  [whole(): pl.pallas_call(functools.partial(kernel, nx, ny, nz, chunks, cap), out_sh...]
    unnamed x15 -> x13, local copies, waits for them, and re-layouts: 4.27 us -> 7.64 us
    reduce_sum x4 -> x0, other arithmetic: 3.12 us -> none  [the longest x1 0.91 us: on_device(): rank = jnp.sum(same & (ids[None, :] < ids[:, None]), axis=1)]
    transpose x1 -> x0, local copies, waits for them, and re-layouts: 2.85 us -> none  [on_device(): hidden_grad.reshape(ny, nz, cap, units).transpose(1, 0, 2, 3)]
    reshape x1 -> x0, local copies, waits for them, and re-layouts: 2.71 us -> none  [on_device(): saved_hidden.reshape(nz, ny, cap, units).transpose(1, 0, 2, 3)]
    convert_element_type x2 -> x0, other arithmetic: 1.93 us -> none  [the longest x1 1.24 us: on_device(): (slot_expert[None, :] == jnp.arange(HOT, dtype=jnp.int32)[:, None]).astyp...]
where the time goes in v3:
time: 160 us
  Pallas kernels  151 us (94%)
  local copies, waits for them, and re-layouts  7.64 us (5%)
    pallas_call x1, Pallas kernels, whole(): pl.pallas_call(functools.partial(kernel, nx, ny, nz, chunks, cap), out_sh...  151 us
    unnamed x13, local copies, waits for them, and re-layouts  7.64 us

profile of v3, /device:TPU:2, one launch (start us, length us, event | category | flops | bytes accessed | tf_op | source)
XLA Modules:
  0.0 159.6 jit_solution(9778986592165817707)
XLA Ops:
  0.6 151.3 %shard_map.128 = (bf16[8,4,24,1024]{3,2,1,0:T(8,128)(2,1)}, f32[4,128]{1,0:T(4,128)}, f32[128,3584]{1,0:T(8,128)}, bf16[128,3584]{1,0:T(8,128)(2,1)}, bf16[128,3584]{1,0:T(8,128)(2,1)}) custom-call(s32[32]{0:T(128)} %holder.1, s32[4,128]{1,0:T(4,128)} %bitcast.23, s32[4,128]{1,0:T(4,128)} %bitcast.24, f32[4,128]{1,0:T(4,128)} %bitcast.25, ...), custom_call_target="tpu_custom_call" | custom-call | flops 11274289152 | bytes 20971520 | tf_op jit(solution)/shard_map/pallas_call | solution.py:729
  151.9 0.0 copy-start.3
  151.9 0.0 copy-start
  152.0 2.8 %copy.20 = bf16[1,1,32,1,24,1024]{5,4,3,2,1,0:T(8,128)(2,1)} copy(bf16[1,1,32,1,24,1024]{5,4,3,2,1,0:T(8,128)(2,1)} %bitcast.15) | data formatting | bytes 3145728
  154.8 0.0 copy-done.3
  154.8 0.6 copy.21
  155.3 0.0 copy-done
  155.3 0.0 copy-start.2
  155.3 1.2 copy.22
  156.6 0.6 copy-done.2
  157.2 0.0 copy-start.1
  157.2 0.9 copy.23
  158.1 0.6 copy-done.1
  158.7 0.9 copy.24
Async XLA Ops:
  151.9 2.8 %copy-start.3 = (f32[4,128]{1,0:T(4,128)S(1)}, f32[4,128]{1,0:T(4,128)}, u32[]{:S(2)}) copy-start(f32[4,128]{1,0:T(4,128)} %get-tuple-element.11) | copy-start | bytes 6148
  151.9 3.4 %copy-start = (f32[128,3584]{1,0:T(8,128)S(1)}, f32[128,3584]{1,0:T(8,128)}, u32[]{:S(2)}) copy-start(f32[128,3584]{1,0:T(8,128)} %get-tuple-element.12) | copy-start | bytes 5505028
  155.3 1.8 %copy-start.2 = (bf16[128,3584]{1,0:T(8,128)(2,1)S(1)}, bf16[128,3584]{1,0:T(8,128)(2,1)}, u32[]{:S(2)}) copy-start(bf16[128,3584]{1,0:T(8,128)(2,1)} %get-tuple-element.13) | copy-start | bytes 2752516
  157.2 1.5 copy-start.1

commit v4 on v3

--- a/solution.py
+++ b/solution.py
@@ -244,8 +244,8 @@
         here = pl.ds(*pieces[i])
         return remote(wg.at[here, c], wg.at[here, c], wcs.at[i], wcr.at[i], other, q)
 
-    def row_copy(j, k, slot):
-        return remote(sendy.at[slot, at_y[j]], rows.at[k, y], ys.at[k], yr.at[k], p, to_y[j])
+    def row_copy(j, k, slot, here):
+        return remote(sendy.at[slot, at_y[j], here], rows.at[k, y, here], ys.at[k], yr.at[k], p, to_y[j])
 
     def row_all(k):
         most = pl.ds(0, ny - 1)
@@ -454,22 +454,27 @@
             lax.fori_loop(0, ny * block // 128, turn, 0)
             proj[...] = jnp.zeros_like(proj)
 
-        @when(tau - picked)
-        def _(k=tau - picked):
-            slot = lax.rem(k, SLACK + 1)
-
-            def choose(jj, carry):
+        def arrived(i, carry):
+            h = far - i
+            side = 2 * lax.rem(z, 2) - 1
+            off = jnp.where(h == 1, 0, jnp.where(h == 2, side, jnp.where(h == 3, -side, 2)))
+            jj = lax.rem(z // 2 + off + nz // 2, nz // 2)
+
+            @when(tau - AHEAD - h)
+            def _(k=tau - AHEAD - h):
+                slot = lax.rem(k, far + SLACK)
                 two = xg[k, pl.ds(2 * jj, 2)].reshape(2 * toks, dk)
                 got = jnp.dot(pick2[jj], two, preferred_element_type=F32).astype(BF)
                 here = pl.ds(pl.multiple_of(jj * pair, pair), pair)
                 for yy in range(ny):
                     sendy[slot, yy, here, :] = got[yy * pair : (yy + 1) * pair, :]
-                return carry
-
-            lax.fori_loop(0, nz // 2, choose, 0)
-            for j in range(1, ny):
-                row_copy(j, k, slot).start()
-            rows[k, y] = sendy[slot, y]
+                for j in range(1, ny):
+                    row_copy(j, k, slot, here).start()
+                rows[k, y, here, :] = sendy[slot, y, here, :]
+
+            return carry
+
+        lax.fori_loop(0, far, arrived, 0)
 
         @grouped(tau - picked - 5 * SLACK)
         def _(k0, n):
@@ -667,7 +672,7 @@
         pltpu.VMEM((nz, 8, toks), F32),
         pltpu.VMEM((chunks, nz, toks, dk), BF),
         pltpu.VMEM((chunks, CORES, nx, shard, dk), BF),
-        pltpu.VMEM((SLACK + 1, ny, block, dk), BF),
+        pltpu.VMEM((nz // 2 + SLACK, ny, block, dk), BF),
         pltpu.VMEM((chunks, ny, block, dk), BF),
         pltpu.VMEM((nz // 2, ny * 2 * cap, 2 * toks), BF),
         pltpu.VMEM((count, 128), F32),

time: 160 us -> 156 us (0.975)
  Pallas kernels: 151 us -> 146 us
    pallas_call x1, Pallas kernels: 151 us -> 146 us  [whole(): pl.pallas_call(functools.partial(kernel, nx, ny, nz, chunks, cap), out_sh...]
where the time goes in v4:
time: 156 us; the launch traced here: 155 us
  Pallas kernels  146 us (94%)
  local copies, waits for them, and re-layouts  7.64 us (5%)
    pallas_call x1, Pallas kernels, whole(): pl.pallas_call(functools.partial(kernel, nx, ny, nz, chunks, cap), out_sh...  146 us
    unnamed x13, local copies, waits for them, and re-layouts  7.64 us

profile of v4, /device:TPU:2, one launch (start us, length us, event | category | flops | bytes accessed | tf_op | source)
XLA Modules:
  0.0 154.7 jit_solution(2506443989772697188)
XLA Ops:
  0.6 146.4 %shard_map.128 = (bf16[8,4,24,1024]{3,2,1,0:T(8,128)(2,1)}, f32[4,128]{1,0:T(4,128)}, f32[128,3584]{1,0:T(8,128)}, bf16[128,3584]{1,0:T(8,128)(2,1)}, bf16[128,3584]{1,0:T(8,128)(2,1)}) custom-call(s32[32]{0:T(128)} %holder.1, s32[4,128]{1,0:T(4,128)} %bitcast.23, s32[4,128]{1,0:T(4,128)} %bitcast.24, f32[4,128]{1,0:T(4,128)} %bitcast.25, ...), custom_call_target="tpu_custom_call" | custom-call | flops 11274289152 | bytes 20971520 | tf_op jit(solution)/shard_map/pallas_call | solution.py:734
  147.1 0.0 copy-start.3
  147.1 0.0 copy-start
  147.1 2.8 %copy.20 = bf16[1,1,32,1,24,1024]{5,4,3,2,1,0:T(8,128)(2,1)} copy(bf16[1,1,32,1,24,1024]{5,4,3,2,1,0:T(8,128)(2,1)} %bitcast.15) | data formatting | bytes 3145728
  149.9 0.0 copy-done.3
  149.9 0.6 copy.21
  150.5 0.0 copy-done
  150.5 0.0 copy-start.2
  150.5 1.2 copy.22
  151.7 0.6 copy-done.2
  152.3 0.0 copy-start.1
  152.3 0.9 copy.23
  153.2 0.6 copy-done.1
  153.8 0.9 copy.24
Async XLA Ops:
  147.1 2.8 %copy-start.3 = (f32[4,128]{1,0:T(4,128)S(1)}, f32[4,128]{1,0:T(4,128)}, u32[]{:S(2)}) copy-start(f32[4,128]{1,0:T(4,128)} %get-tuple-element.11) | copy-start | bytes 6148
  147.1 3.4 %copy-start = (f32[128,3584]{1,0:T(8,128)S(1)}, f32[128,3584]{1,0:T(8,128)}, u32[]{:S(2)}) copy-start(f32[128,3584]{1,0:T(8,128)} %get-tuple-element.12) | copy-start | bytes 5505028
  150.5 1.8 %copy-start.2 = (bf16[128,3584]{1,0:T(8,128)(2,1)S(1)}, bf16[128,3584]{1,0:T(8,128)(2,1)}, u32[]{:S(2)}) copy-start(bf16[128,3584]{1,0:T(8,128)(2,1)} %get-tuple-element.13) | copy-start | bytes 2752516
  152.3 1.5 copy-start.1
